TPU v7x, 32 devices: a whole 2x2x4 slice. The times are simulated.
32 devices in a mesh: grp: 2 (over x), blk: 16 (over z, y, core).
Axes of the slice: x: 2, y: 2, z: 4, core: 2. Of those that a mesh axis runs over, the one named last changes fastest.
Arguments:
- slab: bfloat16 [64, 4, 1, 2, 256, 256], P(('grp', 'blk')), parts along dimension 0, may hold values from -6 to 6
- slab_cols: int32 [32, 4], P('blk'), may hold values from 0 to 31, as said below
- panels: bfloat16 [64, 4, 1, 2, 256, 256], P(('grp', 'blk')), parts along dimension 0, may hold values from -0.25 to 0.25
- panel_rows: int32 [32, 4], P('blk'), may hold values from 0 to 31, as said below
- panel_live: int32 [32], P('blk'), may hold values from 1 to 4, as said below
Outputs:
- multiples: bfloat16 [64, 1, 2, 256, 2560], P(('grp', 'blk')), parts along dimension 0
There are 2 independent parts, one for each index of `grp`. A program takes and returns all parts, laid end to end along the dimension named above; an argument that names none is the same for every part. Nothing has to cross between parts.
Inputs may be any that keep to these rules, and one draw needn't show every extreme that they name: `slab_cols`: within a row panel r the entries are distinct, each within cycle distance 4 (modulo 32) of 2 * (r // 2) + 1. `panel_rows`: within a column panel c the entries are distinct, each within cycle distance 4 (modulo 32) of 2 * (c // 2) + 1; slots from panel_live[c] on hold no data. `panel_live`: some column panel has all 4 slots live.
All inputs are finite; a program needn't handle non-finite values.
Results may differ from a plain program's by a relative error of at most 0.001.
Values may be sent and summed in bfloat16 or wider, within the bound.
No kernel may reach another device: no remote copies, remote signals or barrier semaphores. Data moves between devices by JAX's collectives and lax.ppermute only.
A program may use at most 128 MiB of HBM per device.

v0:
```python
import jax
import jax.numpy as jnp
from jax import lax
from jax.sharding import PartitionSpec as P

HALF = 2


def shifted(block, axis, distance):
    devices = range(lax.axis_size(axis))
    route = [((i - distance) % len(devices), i) for i in devices]
    return lax.ppermute(block, axis, route)


def lifted_blocks(slab_blocks, slab_index, panel_index, panel_count):
    slot_ids = jnp.arange(panel_index.shape[1], dtype=jnp.int32)
    live_slots = slot_ids[None, :] < panel_count[:, None]
    matches = (panel_index[None, :, :, None] == slab_index[:, None, None, :]) & live_slots[
        None, :, :, None
    ]
    lifted = jnp.einsum(
        "rcji,rifpax->rcjfpax",
        matches.astype(jnp.bfloat16),
        slab_blocks,
        preferred_element_type=jnp.float32,
    )
    return lifted.astype(jnp.bfloat16)


def block_products(slab_blocks, slab_index, panel_blocks, panel_index, panel_count):
    lifted = lifted_blocks(slab_blocks, slab_index, panel_index, panel_count)
    real_part = lifted[:, :, :, :, 0]
    imag_part = lifted[:, :, :, :, 1]
    stacked = jnp.stack(
        [jnp.stack([real_part, -imag_part], 3), jnp.stack([imag_part, real_part], 3)], 3
    )
    product = jnp.einsum(
        "rcjopfax,cjfpxb->rfoacb", stacked, panel_blocks, preferred_element_type=jnp.float32
    )
    columns_total = product.shape[4] * product.shape[5]
    return product.reshape(product.shape[0], product.shape[1], 2, product.shape[3], columns_total)


def shards(slab, slab_cols, panels, panel_rows, panel_live):
    results = {0: block_products(slab, slab_cols, panels, panel_rows, panel_live)}
    ahead = (panels, panel_rows, panel_live)
    behind = (panels, panel_rows, panel_live)
    for offset in range(1, HALF + 1):
        ahead = shifted((ahead[0], ahead[1], ahead[2]), "blk", -1)
        behind = shifted((behind[0], behind[1], behind[2]), "blk", 1)
        results[offset] = block_products(slab, slab_cols, ahead[0], ahead[1], ahead[2])
        results[-offset] = block_products(slab, slab_cols, behind[0], behind[1], behind[2])
    ordered = [results[offset].astype(jnp.bfloat16) for offset in range(-HALF, HALF + 1)]
    return jnp.concatenate(ordered, axis=4)


def solution(mesh):
    placed = (
        P(("grp", "blk"), None, None, None, None, None),
        P("blk", None),
        P(("grp", "blk"), None, None, None, None, None),
        P("blk", None),
        P("blk"),
    )
    return jax.shard_map(
        shards,
        mesh=mesh,
        in_specs=placed,
        out_specs=P(("grp", "blk"), None, None, None, None),
        check_vma=False,
    )
```

profile of v0, /device:TPU:1, one launch (start us, length us, event | category | flops | bytes accessed | tf_op | source)
XLA Modules:
  0.0 213.4 jit_solution(16561948462438872260)
XLA Ops:
  0.0 2.7 %collective-permute-start = (s32[2,4]{1,0:T(2,128)}, s32[2,4]{1,0:T(2,128)S(1)}, u32[]{:S(2)}, u32[]{:S(2)}) collective-permute-start(s32[2,4]{1,0:T(2,128)} %param.8), channel_id=1, source_target_pairs={{15,0},{0,1},{1,2},{2,3},{3,4},{4,5},{5,6},{6,7},{7,8},{8,9},{9,10... | collective-permute-start | bytes 104 | tf_op jit(solution)/shard_map/ppermute | solution.py:12
  5.6 4.1 %copy.38 = bf16[2,4,1,2,256,256]{4,5,3,1,0,2:T(8,128)(2,1)} copy(bf16[2,4,1,2,256,256]{5,4,3,2,1,0:T(8,128)(2,1)} %param.7) | data formatting | bytes 4194304 | tf_op args[2]
  15.8 3.0 %maximum_bitcast_fusion.10 = bf16[2,2,4,1,2,1,256,256]{7,2,6,1,0,4,5,3:T(4,128)(2,1)S(1)} fusion(bf16[2,2,4,1,1,256,256]{6,2,5,4,1,0,3:T(4,128)(2,1)S(1)} %get-tuple-element.13, bf16[2,2,4,1,1,256,256]{6,2,5,4,1,0,3:T(4,128)(2,1)S(1)} %get-tuple-element.12), kind=kLoop, calls=%fused_computation.20 | loop fusion | flops 2097152 | bytes 8388608 | tf_op jit(solution)/shard_map/stack | solution.py:34
  18.8 3.0 %maximum_bitcast_fusion.9 = bf16[2,2,4,1,2,1,256,256]{7,2,6,1,0,4,5,3:T(4,128)(2,1)S(1)} fusion(bf16[2,2,4,1,1,256,256]{6,2,5,1,0,3,4:T(4,128)(2,1)S(1)} %bitcast_negate_fusion.2, bf16[2,2,4,1,1,256,256]{6,2,5,1,0,3,4:T(4,128)(2,1)S(1)} %get-tuple-element.11), kind=kLoop, calls=%fused_computation.19 | loop fusion | flops 2097152 | bytes 8388608 | tf_op jit(solution)/shard_map/stack | solution.py:34
  21.8 6.4 %maximum_bitcast_fusion.2 = bf16[2,2,4,2,2,256,256]{6,2,5,1,0,4,3:T(4,128)(2,1)S(1)} fusion(bf16[2,2,4,1,2,1,256,256]{7,2,6,1,0,4,5,3:T(4,128)(2,1)S(1)} %maximum_bitcast_fusion.10, bf16[2,2,4,1,2,1,256,256]{7,2,6,1,0,4,5,3:T(4,128)(2,1)S(1)} %maximum_bitcast_fusion.9), kind=kLoop, calls=%fused_computation.2 | loop fusion | flops 4194304 | bytes 16777216 | tf_op jit(solution)/shard_map/reshape.18
  28.2 4.0 %fusion.45 = bf16[2,1,2,256,2,256]{3,5,2,0,4,1:T(8,128)(2,1)S(1)} fusion(bf16[2,4,1,2,256,256]{5,4,3,2,1,0:T(8,128)(2,1)} %param.7, bf16[2,2,4,2,2,256,256]{6,2,5,1,0,4,3:T(4,128)(2,1)S(1)} %maximum_bitcast_fusion.2), kind=kOutput, calls=%fused_computation.47 | convolution fusion | flops 2148007936 | bytes 11534336 | tf_op jit(solution)/shard_map/rcjopfax,cjfpxb->rfoacb/dot_general | solution.py:37
  32.3 3.9 %collective-permute-start.8 = (bf16[2,4,1,2,256,256]{4,5,3,1,0,2:T(8,128)(2,1)}, bf16[2,4,1,2,256,256]{4,5,3,1,0,2:T(8,128)(2,1)}, u32[]{:S(2)}, u32[]{:S(2)}) collective-permute-start(bf16[2,4,1,2,256,256]{4,5,3,1,0,2:T(8,128)(2,1)} %copy.38), channel_id=1, source_target_pairs={{1,0},{2,1},{3,2},{4,3},{5,4},{6,5},{7,6},{8,7},{9,8},{10,9},{11,1... | collective-permute-start | bytes 6291464 | tf_op jit(solution)/shard_map/ppermute | solution.py:12
  36.4 5.0 %collective-permute-done.3 = s32[2]{0:T(128)S(1)} collective-permute-done((s32[2]{0:T(128)S(1)}, s32[2]{0:T(128)S(1)}, u32[]{:S(2)}, u32[]{:S(2)}) %collective-permute-start.3) | collective-permute-done | bytes 40 | tf_op jit(solution)/shard_map/ppermute | solution.py:12
  41.4 5.2 %collective-permute-start.10 = (s32[2]{0:T(128)S(1)}, s32[2]{0:T(128)S(1)}, u32[]{:S(2)}, u32[]{:S(2)}) collective-permute-start(s32[2]{0:T(128)S(1)} %collective-permute-done.7), channel_id=1, source_target_pairs={{1,0},{2,1},{3,2},{4,3},{5,4},{6,5},{7,6},{8,7},{9,8},{10,9},{11,1... | collective-permute-start | bytes 32 | tf_op jit(solution)/shard_map/ppermute | solution.py:12
  46.7 17.8 %collective-permute-done.10 = s32[2]{0:T(128)S(1)} collective-permute-done((s32[2]{0:T(128)S(1)}, s32[2]{0:T(128)S(1)}, u32[]{:S(2)}, u32[]{:S(2)}) %collective-permute-start.10) | collective-permute-done | bytes 40 | tf_op jit(solution)/shard_map/ppermute | solution.py:12
  69.8 2.5 %convert_bitcast_fusion.1 = bf16[2,2,4,1,2,256,256]{6,2,5,4,1,0,3:T(4,128)(2,1)S(1)} fusion(bf16[2,4,2,256,256,1]{4,3,2,1,0,5:T(8,128)(2,1)S(1)} %bitcast.224, s32[2,4]{1,0:T(2,128)S(1)} %collective-permute-done.6, s32[2,4]{1,0:T(2,128)S(1)} %copy-done.3, pred[2,4]{1,0:T(4,128)(4,1)S(1)} %iota_compare_fusion.1), kind=kOutput, calls=%fused_computation.26 | convolution fusion | flops 18874496 | bytes 6291528 | tf_op jit(solution)/shard_map/rcji,rifpax->rcjfpax/dot_general | solution.py:21
  76.8 3.0 %maximum_bitcast_fusion.8 = bf16[2,2,4,1,2,1,256,256]{7,2,6,1,0,4,5,3:T(4,128)(2,1)S(1)} fusion(bf16[2,2,4,1,1,256,256]{6,2,5,4,1,0,3:T(4,128)(2,1)S(1)} %get-tuple-element.16, bf16[2,2,4,1,1,256,256]{6,2,5,4,1,0,3:T(4,128)(2,1)S(1)} %get-tuple-element.15), kind=kLoop, calls=%fused_computation.18 | loop fusion | flops 2097152 | bytes 8388608 | tf_op jit(solution)/shard_map/stack | solution.py:34
  79.8 3.0 %maximum_bitcast_fusion.7 = bf16[2,2,4,1,2,1,256,256]{7,2,6,1,0,4,5,3:T(4,128)(2,1)S(1)} fusion(bf16[2,2,4,1,1,256,256]{6,2,5,1,0,3,4:T(4,128)(2,1)S(1)} %bitcast_negate_fusion.3, bf16[2,2,4,1,1,256,256]{6,2,5,1,0,3,4:T(4,128)(2,1)S(1)} %get-tuple-element.14), kind=kLoop, calls=%fused_computation.17 | loop fusion | flops 2097152 | bytes 8388608 | tf_op jit(solution)/shard_map/stack | solution.py:34
  82.7 7.5 %maximum_bitcast_fusion.1 = bf16[2,2,4,2,2,256,256]{6,2,5,1,0,4,3:T(4,128)(2,1)} fusion(bf16[2,2,4,1,2,1,256,256]{7,2,6,1,0,4,5,3:T(4,128)(2,1)S(1)} %maximum_bitcast_fusion.8, bf16[2,2,4,1,2,1,256,256]{7,2,6,1,0,4,5,3:T(4,128)(2,1)S(1)} %maximum_bitcast_fusion.7), kind=kLoop, calls=%fused_computation.1 | loop fusion | flops 4194304 | bytes 16777216 | tf_op jit(solution)/shard_map/reshape.13
  90.3 3.0 %maximum_bitcast_fusion.12 = bf16[2,2,4,1,2,1,256,256]{7,2,6,1,0,4,5,3:T(4,128)(2,1)S(1)} fusion(bf16[2,2,4,1,1,256,256]{6,2,5,4,1,0,3:T(4,128)(2,1)S(1)} %get-tuple-element.10, bf16[2,2,4,1,1,256,256]{6,2,5,4,1,0,3:T(4,128)(2,1)S(1)} %get-tuple-element.9), kind=kLoop, calls=%fused_computation.22 | loop fusion | flops 2097152 | bytes 8388608 | tf_op jit(solution)/shard_map/stack | solution.py:34
  93.3 3.0 %maximum_bitcast_fusion.11 = bf16[2,2,4,1,2,1,256,256]{7,2,6,1,0,4,5,3:T(4,128)(2,1)S(1)} fusion(bf16[2,2,4,1,1,256,256]{6,2,5,1,0,3,4:T(4,128)(2,1)S(1)} %copy-done.2, bf16[2,2,4,1,1,256,256]{6,2,5,1,0,3,4:T(4,128)(2,1)S(1)} %get-tuple-element.8), kind=kLoop, calls=%fused_computation.21 | loop fusion | flops 2097152 | bytes 8388608 | tf_op jit(solution)/shard_map/stack | solution.py:34
  96.2 7.3 %maximum_bitcast_fusion.3 = bf16[2,2,4,2,2,256,256]{6,2,5,1,0,4,3:T(4,128)(2,1)} fusion(bf16[2,2,4,1,2,1,256,256]{7,2,6,1,0,4,5,3:T(4,128)(2,1)S(1)} %maximum_bitcast_fusion.12, bf16[2,2,4,1,2,1,256,256]{7,2,6,1,0,4,5,3:T(4,128)(2,1)S(1)} %maximum_bitcast_fusion.11), kind=kLoop, calls=%fused_computation.3 | loop fusion | flops 4194304 | bytes 16777216 | tf_op jit(solution)/shard_map/reshape.23
  111.3 2.5 %convert_bitcast_fusion = bf16[2,2,4,1,2,256,256]{6,2,5,4,1,0,3:T(4,128)(2,1)S(1)} fusion(bf16[2,4,2,256,256,1]{4,3,2,1,0,5:T(8,128)(2,1)S(1)} %bitcast.223, s32[2,4]{1,0:T(2,128)S(1)} %collective-permute-done.9, s32[2,4]{1,0:T(2,128)S(1)} %copy-done.3, pred[2,4]{1,0:T(4,128)(4,1)S(1)} %iota_compare_fusion), kind=kOutput, calls=%fused_computation.25 | convolution fusion | flops 18874496 | bytes 6291528 | tf_op jit(solution)/shard_map/rcji,rifpax->rcjfpax/dot_general | solution.py:21
  113.8 3.5 %slice_bitcast_fusion = (bf16[2,2,4,1,1,256,256]{6,2,5,1,0,3,4:T(4,128)(2,1)S(1)}, bf16[2,2,4,1,1,256,256]{6,2,5,4,1,0,3:T(4,128)(2,1)}, bf16[2,2,4,1,1,256,256]{6,2,5,4,1,0,3:T(4,128)(2,1)}) fusion(bf16[2,2,4,1,2,256,256]{6,2,5,4,1,0,3:T(4,128)(2,1)S(1)} %convert_bitcast_fusion), kind=kLoop, calls=%fused_computation.95 | loop fusion | bytes 10485760
  117.3 3.0 %maximum_bitcast_fusion.6 = bf16[2,2,4,1,2,1,256,256]{7,2,6,1,0,4,5,3:T(4,128)(2,1)S(1)} fusion(bf16[2,2,4,1,1,256,256]{6,2,5,4,1,0,3:T(4,128)(2,1)S(1)} %get-tuple-element.19, bf16[2,2,4,1,1,256,256]{6,2,5,4,1,0,3:T(4,128)(2,1)S(1)} %get-tuple-element.18), kind=kLoop, calls=%fused_computation.16 | loop fusion | flops 2097152 | bytes 8388608 | tf_op jit(solution)/shard_map/stack | solution.py:34
  120.3 4.7 %maximum_bitcast_fusion.5 = bf16[2,2,4,1,2,1,256,256]{7,2,6,1,0,4,5,3:T(4,128)(2,1)S(1)} fusion(bf16[2,2,4,1,1,256,256]{6,2,5,1,0,3,4:T(4,128)(2,1)} %bitcast_negate_fusion.4, bf16[2,2,4,1,1,256,256]{6,2,5,1,0,3,4:T(4,128)(2,1)S(1)} %get-tuple-element.17), kind=kLoop, calls=%fused_computation.15 | loop fusion | flops 2097152 | bytes 8388608 | tf_op jit(solution)/shard_map/stack | solution.py:34
  125.0 5.4 %maximum_bitcast_fusion.14 = bf16[2,2,4,1,2,1,256,256]{7,2,6,1,0,4,5,3:T(4,128)(2,1)S(1)} fusion(bf16[2,2,4,1,1,256,256]{6,2,5,4,1,0,3:T(4,128)(2,1)} %get-tuple-element.7, bf16[2,2,4,1,1,256,256]{6,2,5,4,1,0,3:T(4,128)(2,1)} %get-tuple-element.6), kind=kLoop, calls=%fused_computation.24 | loop fusion | flops 2097152 | bytes 8388608 | tf_op jit(solution)/shard_map/stack | solution.py:34
  131.3 3.1 %maximum_bitcast_fusion.13 = bf16[2,2,4,1,2,1,256,256]{7,2,6,1,0,4,5,3:T(4,128)(2,1)S(1)} fusion(bf16[2,2,4,1,1,256,256]{6,2,5,1,0,3,4:T(4,128)(2,1)S(1)} %bitcast_negate_fusion, bf16[2,2,4,1,1,256,256]{6,2,5,1,0,3,4:T(4,128)(2,1)S(1)} %get-tuple-element.5), kind=kLoop, calls=%fused_computation.23 | loop fusion | flops 2097152 | bytes 8388608 | tf_op jit(solution)/shard_map/stack | solution.py:34
  134.4 7.4 %maximum_bitcast_fusion = bf16[2,2,4,2,2,256,256]{6,2,5,1,0,4,3:T(4,128)(2,1)} fusion(bf16[2,2,4,1,2,1,256,256]{7,2,6,1,0,4,5,3:T(4,128)(2,1)S(1)} %maximum_bitcast_fusion.6, bf16[2,2,4,1,2,1,256,256]{7,2,6,1,0,4,5,3:T(4,128)(2,1)S(1)} %maximum_bitcast_fusion.5), kind=kLoop, calls=%fused_computation | loop fusion | flops 4194304 | bytes 16777216 | tf_op jit(solution)/shard_map/reshape.3
  143.6 7.3 %maximum_bitcast_fusion.4 = bf16[2,2,4,2,2,256,256]{6,2,5,1,0,4,3:T(4,128)(2,1)} fusion(bf16[2,2,4,1,2,1,256,256]{7,2,6,1,0,4,5,3:T(4,128)(2,1)S(1)} %maximum_bitcast_fusion.14, bf16[2,2,4,1,2,1,256,256]{7,2,6,1,0,4,5,3:T(4,128)(2,1)S(1)} %maximum_bitcast_fusion.13), kind=kLoop, calls=%fused_computation.4 | loop fusion | flops 4194304 | bytes 16777216 | tf_op jit(solution)/shard_map/reshape.28
  150.9 3.0 %collective-permute-start.11 = (bf16[2,4,1,2,256,256]{4,5,3,1,0,2:T(8,128)(2,1)}, bf16[2,4,1,2,256,256]{4,5,3,1,0,2:T(8,128)(2,1)}, u32[]{:S(2)}, u32[]{:S(2)}) collective-permute-start(bf16[2,4,1,2,256,256]{4,5,3,1,0,2:T(8,128)(2,1)} %collective-permute-done.8), channel_id=1, source_target_pairs={{1,0},{2,1},{3,2},{4,3},{5,4},{6,5},{7,6},{8,7},{9,8},{10,9},{11,1... | collective-permute-start | bytes 6291464 | tf_op jit(solution)/shard_map/ppermute | solution.py:12
  154.0 4.0 %fusion.40 = bf16[2,1,2,256,2,256]{3,5,2,0,4,1:T(8,128)(2,1)S(1)} fusion(bf16[2,4,1,2,256,256]{4,5,3,1,0,2:T(8,128)(2,1)} %collective-permute-done.4, bf16[2,2,4,2,2,256,256]{6,2,5,1,0,4,3:T(4,128)(2,1)S(1)} %bitcast.228), kind=kOutput, calls=%fused_computation.46 | convolution fusion | flops 2148007936 | bytes 11534336 | tf_op jit(solution)/shard_map/rcjopfax,cjfpxb->rfoacb/dot_general | solution.py:37
  158.0 6.4 %fusion.50 = bf16[2,1,2,256,2,256]{3,5,2,0,4,1:T(8,128)(2,1)S(1)} fusion(bf16[2,4,1,2,256,256]{4,5,3,1,0,2:T(8,128)(2,1)} %collective-permute-done.8, bf16[2,2,4,2,2,256,256]{6,2,5,1,0,4,3:T(4,128)(2,1)} %maximum_bitcast_fusion.3), kind=kOutput, calls=%fused_computation.48 | convolution fusion | flops 2148007936 | bytes 11534336 | tf_op jit(solution)/shard_map/rcjopfax,cjfpxb->rfoacb/dot_general | solution.py:37
  164.4 25.0 %collective-permute-done.5 = bf16[2,4,1,2,256,256]{4,5,3,1,0,2:T(8,128)(2,1)} collective-permute-done((bf16[2,4,1,2,256,256]{4,5,3,1,0,2:T(8,128)(2,1)}, bf16[2,4,1,2,256,256]{4,5,3,1,0,2:T(8,128)(2,1)}, u32[]{:S(2)}, u32[]{:S(2)}) %collective-permute-start.5) | collective-permute-done | bytes 2097184 | tf_op jit(solution)/shard_map/ppermute | solution.py:12
  189.4 6.3 %fusion.35 = bf16[2,1,2,256,2,256]{3,5,2,0,4,1:T(8,128)(2,1)S(1)} fusion(bf16[2,4,1,2,256,256]{4,5,3,1,0,2:T(8,128)(2,1)} %collective-permute-done.5, bf16[2,2,4,2,2,256,256]{6,2,5,1,0,4,3:T(4,128)(2,1)} %maximum_bitcast_fusion), kind=kOutput, calls=%fused_computation.45 | convolution fusion | flops 2148007936 | bytes 11534336 | tf_op jit(solution)/shard_map/rcjopfax,cjfpxb->rfoacb/dot_general | solution.py:37
  196.9 4.0 %fusion.55 = bf16[2,1,2,256,2,256]{3,5,2,0,4,1:T(8,128)(2,1)S(1)} fusion(bf16[2,4,1,2,256,256]{4,5,3,1,0,2:T(8,128)(2,1)} %collective-permute-done.11, bf16[2,2,4,2,2,256,256]{6,2,5,1,0,4,3:T(4,128)(2,1)S(1)} %bitcast.230), kind=kOutput, calls=%fused_computation.49 | convolution fusion | flops 2148007936 | bytes 11534336 | tf_op jit(solution)/shard_map/rcjopfax,cjfpxb->rfoacb/dot_general | solution.py:37
  205.3 7.9 %copy.67 = bf16[2,1,2,256,2560]{4,3,2,1,0:T(8,128)(2,1)} copy(bf16[2,1,2,256,2560]{3,4,2,0,1:T(8,128)(2,1)} %constant_dynamic-update-slice_fusion) | data formatting | bytes 10485760 | tf_op jit(solution)/shard_map/concatenate | solution.py:54
  (66 shorter events, 35.2 us)
Async XLA Ops:
  0.0 10.4 %copy-start = (bf16[2,4,1,2,256,256]{5,4,3,2,1,0:T(8,128)(2,1)S(1)}, bf16[2,4,1,2,256,256]{5,4,3,2,1,0:T(8,128)(2,1)}, u32[]{:S(2)}) copy-start(bf16[2,4,1,2,256,256]{5,4,3,2,1,0:T(8,128)(2,1)} %param.5) | copy-start | bytes 6291460
  0.0 10.4 %copy-start.4 = (s32[2,4]{1,0:T(2,128)S(1)}, s32[2,4]{1,0:T(2,128)}, u32[]{:S(2)}) copy-start(s32[2,4]{1,0:T(2,128)} %param.8) | copy-start | bytes 100
  0.0 10.3 %copy-start.5 = (s32[2]{0:T(128)S(1)}, s32[2]{0:T(128)}, u32[]{:S(2)}) copy-start(s32[2]{0:T(128)} %param.9) | copy-start | bytes 28
  0.0 10.4 %copy-start.3 = (s32[2,4]{1,0:T(2,128)S(1)}, s32[2,4]{1,0:T(2,128)}, u32[]{:S(2)}) copy-start(s32[2,4]{1,0:T(2,128)} %param.6) | copy-start | bytes 100
  0.0 64.5 %collective-permute-start = (s32[2,4]{1,0:T(2,128)}, s32[2,4]{1,0:T(2,128)S(1)}, u32[]{:S(2)}, u32[]{:S(2)}) collective-permute-start(s32[2,4]{1,0:T(2,128)} %param.8), channel_id=1, source_target_pairs={{15,0},{0,1},{1,2},{2,3},{3,4},{4,5},{5,6},{6,7},{7,8},{8,9},{9,10... | collective-permute-start | bytes 104 | tf_op jit(solution)/shard_map/ppermute | solution.py:12
  2.7 67.1 %collective-permute-start.6 = (s32[2,4]{1,0:T(2,128)}, s32[2,4]{1,0:T(2,128)S(1)}, u32[]{:S(2)}, u32[]{:S(2)}) collective-permute-start(s32[2,4]{1,0:T(2,128)} %param.8), channel_id=1, source_target_pairs={{1,0},{2,1},{3,2},{4,3},{5,4},{6,5},{7,6},{8,7},{9,8},{10,9},{11,1... | collective-permute-start | bytes 104 | tf_op jit(solution)/shard_map/ppermute | solution.py:12
  2.7 29.6 %collective-permute-start.2 = (s32[2]{0:T(128)}, s32[2]{0:T(128)S(1)}, u32[]{:S(2)}, u32[]{:S(2)}) collective-permute-start(s32[2]{0:T(128)} %param.9), channel_id=1, source_target_pairs={{15,0},{0,1},{1,2},{2,3},{3,4},{4,5},{5,6},{6,7},{7,8},{8,9},{9,10... | collective-permute-start | bytes 32 | tf_op jit(solution)/shard_map/ppermute | solution.py:12
  4.4 31.9 %collective-permute-start.7 = (s32[2]{0:T(128)}, s32[2]{0:T(128)S(1)}, u32[]{:S(2)}, u32[]{:S(2)}) collective-permute-start(s32[2]{0:T(128)} %param.9), channel_id=1, source_target_pairs={{1,0},{2,1},{3,2},{4,3},{5,4},{6,5},{7,6},{8,7},{9,8},{10,9},{11,1... | collective-permute-start | bytes 32 | tf_op jit(solution)/shard_map/ppermute | solution.py:12
  9.8 132.0 %collective-permute-start.4 = (bf16[2,4,1,2,256,256]{4,5,3,1,0,2:T(8,128)(2,1)}, bf16[2,4,1,2,256,256]{4,5,3,1,0,2:T(8,128)(2,1)}, u32[]{:S(2)}, u32[]{:S(2)}) collective-permute-start(bf16[2,4,1,2,256,256]{4,5,3,1,0,2:T(8,128)(2,1)} %copy.38), channel_id=1, source_target_pairs={{15,0},{0,1},{1,2},{2,3},{3,4},{4,5},{5,6},{6,7},{7,8},{8,9},{9,10... | collective-permute-start | bytes 6291464 | tf_op jit(solution)/shard_map/ppermute | solution.py:12
  32.3 118.7 %collective-permute-start.8 = (bf16[2,4,1,2,256,256]{4,5,3,1,0,2:T(8,128)(2,1)}, bf16[2,4,1,2,256,256]{4,5,3,1,0,2:T(8,128)(2,1)}, u32[]{:S(2)}, u32[]{:S(2)}) collective-permute-start(bf16[2,4,1,2,256,256]{4,5,3,1,0,2:T(8,128)(2,1)} %copy.38), channel_id=1, source_target_pairs={{1,0},{2,1},{3,2},{4,3},{5,4},{6,5},{7,6},{8,7},{9,8},{10,9},{11,1... | collective-permute-start | bytes 6291464 | tf_op jit(solution)/shard_map/ppermute | solution.py:12
  36.3 5.1 %collective-permute-start.3 = (s32[2]{0:T(128)S(1)}, s32[2]{0:T(128)S(1)}, u32[]{:S(2)}, u32[]{:S(2)}) collective-permute-start(s32[2]{0:T(128)S(1)} %collective-permute-done.2), channel_id=1, source_target_pairs={{15,0},{0,1},{1,2},{2,3},{3,4},{4,5},{5,6},{6,7},{7,8},{8,9},{9,10... | collective-permute-start | bytes 32 | tf_op jit(solution)/shard_map/ppermute | solution.py:12
  41.4 23.1 %collective-permute-start.10 = (s32[2]{0:T(128)S(1)}, s32[2]{0:T(128)S(1)}, u32[]{:S(2)}, u32[]{:S(2)}) collective-permute-start(s32[2]{0:T(128)S(1)} %collective-permute-done.7), channel_id=1, source_target_pairs={{1,0},{2,1},{3,2},{4,3},{5,4},{6,5},{7,6},{8,7},{9,8},{10,9},{11,1... | collective-permute-start | bytes 32 | tf_op jit(solution)/shard_map/ppermute | solution.py:12
  90.3 3.0 %copy-start.2 = (bf16[2,2,4,1,1,256,256]{6,2,5,1,0,3,4:T(4,128)(2,1)S(1)}, bf16[2,2,4,1,1,256,256]{6,2,5,1,0,3,4:T(4,128)(2,1)}, u32[]{:S(2)}) copy-start(bf16[2,2,4,1,1,256,256]{6,2,5,1,0,3,4:T(4,128)(2,1)} %bitcast_negate_fusion.1) | copy-start | bytes 6291460
  103.5 1.1 collective-permute-start.1
  103.5 7.7 %collective-permute-start.9 = (s32[2,4]{1,0:T(2,128)S(1)}, s32[2,4]{1,0:T(2,128)S(1)}, u32[]{:S(2)}, u32[]{:S(2)}) collective-permute-start(s32[2,4]{1,0:T(2,128)S(1)} %collective-permute-done.6), channel_id=1, source_target_pairs={{1,0},{2,1},{3,2},{4,3},{5,4},{6,5},{7,6},{8,7},{9,8},{10,9},{11,1... | collective-permute-start | bytes 104 | tf_op jit(solution)/shard_map/ppermute | solution.py:12
  134.4 19.5 %slice-start = ((s8[8388608]{0:T(1024)(128)(4,1)}), s8[4194304]{0:T(1024)(128)(4,1)S(1)}, s32[]{:S(2)}) async-start(s8[8388608]{0:T(1024)(128)(4,1)} %bitcast.227), calls=%async_computation | async-start | bytes 8388608
  141.8 12.2 %slice-start.1 = ((s8[8388608]{0:T(1024)(128)(4,1)}), s8[4194304]{0:T(1024)(128)(4,1)S(1)}, s32[]{:S(2)}) async-start(s8[8388608]{0:T(1024)(128)(4,1)} %bitcast.227), calls=%async_computation.1 | async-start | bytes 8388608
  141.8 47.6 %collective-permute-start.5 = (bf16[2,4,1,2,256,256]{4,5,3,1,0,2:T(8,128)(2,1)}, bf16[2,4,1,2,256,256]{4,5,3,1,0,2:T(8,128)(2,1)}, u32[]{:S(2)}, u32[]{:S(2)}) collective-permute-start(bf16[2,4,1,2,256,256]{4,5,3,1,0,2:T(8,128)(2,1)} %collective-permute-done.4), channel_id=1, source_target_pairs={{15,0},{0,1},{1,2},{2,3},{3,4},{4,5},{5,6},{6,7},{7,8},{8,9},{9,10... | collective-permute-start | bytes 6291464 | tf_op jit(solution)/shard_map/ppermute | solution.py:12
  150.9 46.0 %collective-permute-start.11 = (bf16[2,4,1,2,256,256]{4,5,3,1,0,2:T(8,128)(2,1)}, bf16[2,4,1,2,256,256]{4,5,3,1,0,2:T(8,128)(2,1)}, u32[]{:S(2)}, u32[]{:S(2)}) collective-permute-start(bf16[2,4,1,2,256,256]{4,5,3,1,0,2:T(8,128)(2,1)} %collective-permute-done.8), channel_id=1, source_target_pairs={{1,0},{2,1},{3,2},{4,3},{5,4},{6,5},{7,6},{8,7},{9,8},{10,9},{11,1... | collective-permute-start | bytes 6291464 | tf_op jit(solution)/shard_map/ppermute | solution.py:12
  164.3 32.6 %slice-start.2 = ((s8[8388608]{0:T(1024)(128)(4,1)}), s8[4194304]{0:T(1024)(128)(4,1)S(1)}, s32[]{:S(2)}) async-start(s8[8388608]{0:T(1024)(128)(4,1)} %bitcast.229), calls=%async_computation.2 | async-start | bytes 8388608
  164.4 32.5 %slice-start.3 = ((s8[8388608]{0:T(1024)(128)(4,1)}), s8[4194304]{0:T(1024)(128)(4,1)S(1)}, s32[]{:S(2)}) async-start(s8[8388608]{0:T(1024)(128)(4,1)} %bitcast.229), calls=%async_computation.3 | async-start | bytes 8388608
  204.2 9.0 %copy-start.1 = (bf16[2,4,1,2,256,256]{5,4,3,2,1,0:T(8,128)(2,1)S(1)}, bf16[2,4,1,2,256,256]{5,4,3,2,1,0:T(8,128)(2,1)}, u32[]{:S(2)}) copy-start(bf16[2,4,1,2,256,256]{5,4,3,2,1,0:T(8,128)(2,1)} %param.5) | copy-start | bytes 6291460
where the time goes:
time: 217 us; the launch traced here: 213 us
  other arithmetic  77.3 us (36%)
  waiting for transfers between devices  48.4 us (22%)
  matrix products  37.1 us (17%)
  local copies, waits for them, and re-layouts  29.3 us (14%)
  starting transfers between devices  20.7 us (10%)
    ppermute x12, waiting for transfers between devices, shifted(): return lax.ppermute(block, axis, route)  48.4 us
    another operation x5, other arithmetic  35.9 us
    another operation x10, other arithmetic, block_products(): jnp.stack([jnp.stack([real_part, -imag_part], 3), jnp.stack([imag_part, r...  34 us
    dot_general x5, matrix products, block_products(): jnp.einsum('rcjopfax,cjfpxb->rfoacb', stacked, panel_blocks, preferred_el...  24.6 us
    ppermute x12, starting transfers between devices, shifted(): return lax.ppermute(block, axis, route)  20.7 us
    unnamed x30, local copies, waits for them, and re-layouts  20 us
    dot_general x5, matrix products, lifted_blocks(): jnp.einsum('rcji,rifpax->rcjfpax', matches.astype(jnp.bfloat16), slab_blo...  12.5 us
    concatenate x2, local copies, waits for them, and re-layouts, shards(): return jnp.concatenate(ordered, axis=4)  9.01 us
  transfers between devices with their start and end apart: 12, of which 4 were waited for; matrix products, arithmetic and copies ran while one was open for 60% of the time, Pallas kernels for 0%

commit v1 on v0

v1 whole, which is shorter than its diff:
```python
import functools

import jax
import jax.numpy as jnp
from jax import lax
from jax.experimental import pallas as pl
from jax.experimental.pallas import tpu as pltpu
from jax.sharding import PartitionSpec as P

HALF = 2
CHUNKS = (2, 2, 2, 2)


def product_kernel(groups, arrays, slots, aliased, *refs):
    match_ref, place_ref, slab_ref = refs[:3]
    chunk_refs = refs[3 : 3 + arrays]
    refs = refs[3 + arrays + aliased :]
    out_ref, slab_v, block_v, total, out_v, slab_sem, block_sem, out_sem = refs
    rows, _, freqs = slab_ref.shape[:3]
    side = slab_ref.shape[4]
    sources = [ref.at[i] for ref in chunk_refs for i in range(ref.shape[0])]

    def needed(b):
        hit = match_ref[b * rows] >= 0
        for r in range(1, rows):
            hit = jnp.logical_or(hit, match_ref[b * rows + r] >= 0)
        return hit

    slab_copy = pltpu.make_async_copy(slab_ref, slab_v, slab_sem)
    slab_copy.start()
    for b, source in enumerate(sources):

        @pl.when(needed(b))
        def _():
            pltpu.make_async_copy(source, block_v.at[b], block_sem.at[b]).start()

    slab_copy.wait()

    def out_copy(g, r):
        return pltpu.make_async_copy(
            out_v.at[g, r],
            out_ref.at[r, :, :, :, pl.ds(pl.multiple_of(place_ref[g] * side, side), side)],
            out_sem.at[g, r],
        )

    def group(g, carry):
        total[...] = jnp.zeros_like(total)

        def slot(j, carry):
            b = g * slots + j

            @pl.when(needed(b))
            def _():
                pltpu.make_async_copy(block_v.at[b], block_v.at[b], block_sem.at[b]).wait()

            for r in range(rows):
                own = match_ref[b * rows + r]

                @pl.when(own >= 0)
                def _():
                    dot = functools.partial(jnp.dot, preferred_element_type=jnp.float32)
                    for f in range(freqs):
                        real, imag = slab_v[r, own, f, 0], slab_v[r, own, f, 1]
                        b_real, b_imag = block_v[b, f, 0], block_v[b, f, 1]
                        total[r, f, 0] += dot(real, b_real) - dot(imag, b_imag)
                        total[r, f, 1] += dot(real, b_imag) + dot(imag, b_real)

            return carry

        lax.fori_loop(0, slots, slot, 0)
        for r in range(rows):
            out_v[g, r] = total[r].astype(out_v.dtype)
            out_copy(g, r).start()
        return carry

    lax.fori_loop(0, groups, group, 0)

    def drain(g, carry):
        for r in range(rows):
            out_copy(g, r).wait()
        return carry

    lax.fori_loop(0, groups, drain, 0)


def products(slab, match, place, chunks, out_shape, before=None):
    rows, _, freqs, parts, side, _ = slab.shape
    groups = place.shape[0]
    slots = sum(chunk.shape[0] for chunk in chunks) // groups
    any_spec = pl.BlockSpec(memory_space=pl.ANY)
    smem_spec = pl.BlockSpec(memory_space=pltpu.SMEM)
    operands = [match, place, slab, *chunks] + ([] if before is None else [before])
    return pl.pallas_call(
        functools.partial(product_kernel, groups, len(chunks), slots, before is not None),
        out_shape=out_shape,
        in_specs=[smem_spec, smem_spec] + [any_spec] * (len(operands) - 2),
        out_specs=any_spec,
        scratch_shapes=[
            pltpu.VMEM(slab.shape, slab.dtype),
            pltpu.VMEM((groups * slots, freqs, parts, side, side), slab.dtype),
            pltpu.VMEM((rows, freqs, parts, side, side), jnp.float32),
            pltpu.VMEM((groups, rows, freqs, parts, side, side), out_shape.dtype),
            pltpu.SemaphoreType.DMA,
            pltpu.SemaphoreType.DMA((groups * slots,)),
            pltpu.SemaphoreType.DMA((groups, rows)),
        ],
        input_output_aliases={} if before is None else {len(operands) - 1: 0},
        compiler_params=pltpu.CompilerParams(vmem_limit_bytes=32 * 2**20),
        cost_estimate=pl.CostEstimate(
            flops=groups * slots * rows * 4 * freqs * side**3,
            bytes_accessed=2 * (slab.size + groups * (slots + rows) * freqs * parts * side * side),
            transcendentals=0,
        ),
    )(*operands)


def shards(slab, slab_cols, panels, panel_rows, panel_live):
    rows, _, freqs, parts, side, _ = slab.shape
    cols, slots = panel_rows.shape
    devices = lax.axis_size("blk")
    me = lax.axis_index("blk")
    core, odd = me % 2, (me // 2) % 2

    def permuted(value, target):
        return lax.ppermute(value, "blk", [(i, target(i)) for i in range(devices)])

    def partner_chip(i):
        return i ^ 2

    def partner_core(i):
        return i ^ 1

    def onward(i):
        return (i + 4 if (i // 2) % 2 == 0 else i - 4) % devices

    live = jnp.arange(slots, dtype=jnp.int32)[None, :] < panel_live[:, None]
    own_rows = jnp.where(live, panel_rows, -1)

    blocks = panels.reshape((cols * slots,) + panels.shape[2:])
    edges = [sum(CHUNKS[:k]) for k in range(len(CHUNKS) + 1)]
    pieces = [blocks[a:b] for a, b in zip(edges[:-1], edges[1:])]
    across, along, passed = [], [], []
    sends_across = core == odd

    for k in range(len(pieces)):
        if k >= 2:
            across[k - 2], pieces[k] = lax.optimization_barrier((across[k - 2], pieces[k]))
        across.append(permuted(pieces[k], partner_chip))
    swapped = permuted(blocks, partner_core)
    for k in range(len(pieces)):
        along.append(permuted(across[k], onward))
    for k in range(len(pieces)):
        handed = jnp.where(sends_across, across[k], along[k])
        passed.append(permuted(handed, partner_core))

    rows_of = {0: own_rows}
    for s in (1, -1, 2, -2):
        rows_of[s] = permuted(own_rows, lambda i, s=s: (i - s) % devices)

    def matches(s, g_rows):
        same = g_rows[:, :, None, None] == slab_cols[None, None, :, :]
        index = jnp.arange(same.shape[-1], dtype=jnp.int32)
        return jnp.max(jnp.where(same, index, -1), axis=-1).reshape(-1)

    out_shape = jax.ShapeDtypeStruct(
        (rows, freqs, parts, side, (2 * HALF + 1) * cols * side), jnp.bfloat16
    )
    q = jnp.arange(cols, dtype=jnp.int32)

    def step(sources, before):
        match = jnp.concatenate([matches(s, r) for s, r, _ in sources])
        place = jnp.concatenate([(s + HALF) * cols + q for s, _, _ in sources])
        chunks = [c for _, _, cs in sources for c in cs]
        return products(slab, match, place, chunks, out_shape, before)

    side_near = jnp.where(core == 0, 1, -1)
    rows_near = jnp.where(core == 0, rows_of[1], rows_of[-1])
    rows_far = jnp.where(core == 0, rows_of[-1], rows_of[1])
    side_across = jnp.where(odd == 0, 2, -2)
    rows_across = jnp.where(odd == 0, rows_of[2], rows_of[-2])
    rows_along = jnp.where(odd == 0, rows_of[-2], rows_of[2])

    out = step([(0, own_rows, [blocks]), (side_near, rows_near, [swapped])], None)
    out = step([(side_across, rows_across, across)], out)
    out = step([(-side_across, rows_along, along), (-side_near, rows_far, passed)], out)
    return out


def solution(mesh):
    placed = (
        P(("grp", "blk"), None, None, None, None, None),
        P("blk", None),
        P(("grp", "blk"), None, None, None, None, None),
        P("blk", None),
        P("blk"),
    )
    return jax.shard_map(
        shards,
        mesh=mesh,
        in_specs=placed,
        out_specs=P(("grp", "blk"), None, None, None, None),
        check_vma=False,
    )
```

time: 217 us -> 92.9 us (0.43); the launches traced: 213 us -> 93 us
  other arithmetic: 77.3 us -> 1.9 us
  matrix products: 37.1 us -> 0 us
  local copies, waits for them, and re-layouts: 29.3 us -> 3.64 us
  Pallas kernels: 0 us -> 13.7 us
  waiting for transfers between devices: 48.4 us -> 60.5 us
  starting transfers between devices: 20.7 us -> 13.2 us
    another operation x15 -> x0, other arithmetic: 69.9 us -> none
    dot_general x10 -> x0, matrix products: 37.1 us -> none  [the longest x5 24.6 us: block_products(): jnp.einsum('rcjopfax,cjfpxb->rfoacb', stacked, panel_blocks, preferred_el...]
    unnamed x30 -> x10, local copies, waits for them, and re-layouts: 20 us -> 0.02 us
    pallas_call x0 -> x3, Pallas kernels: none -> 13.7 us  [products(): pl.pallas_call(functools.partial(product_kernel, groups, len(chunks), slo...]
    ppermute x12 -> x17, waiting for transfers between devices: 48.4 us -> 60.5 us  [permuted(): return lax.ppermute(value, 'blk', [(i, target(i)) for i in range(devices)])]
    concatenate x2 -> x0, local copies, waits for them, and re-layouts: 9.01 us -> none  [shards(): return jnp.concatenate(ordered, axis=4)]
    ppermute x12 -> x17, starting transfers between devices: 20.7 us -> 13.2 us  [permuted(): return lax.ppermute(value, 'blk', [(i, target(i)) for i in range(devices)])]
    neg x5 -> x0, other arithmetic: 7.05 us -> none  [block_products(): -imag_part]
  transfers between devices with their start and end apart: 12 -> 17, of which waited for: 4 -> 7; matrix products, arithmetic and copies ran while one was open for 60% -> 5% of each run, Pallas kernels for 0% -> 9%
where the time goes in v1:
time: 92.9 us; the launch traced here: 93 us
  waiting for transfers between devices  60.5 us (65%)
  Pallas kernels  13.7 us (15%)
  starting transfers between devices  13.2 us (14%)
  local copies, waits for them, and re-layouts  3.64 us (4%)
  other arithmetic  1.9 us (2%)
    ppermute x17, waiting for transfers between devices, permuted(): return lax.ppermute(value, 'blk', [(i, target(i)) for i in range(devices)])  60.5 us
    pallas_call x3, Pallas kernels, products(): pl.pallas_call(functools.partial(product_kernel, groups, len(chunks), slo...  13.7 us
    ppermute x17, starting transfers between devices, permuted(): return lax.ppermute(value, 'blk', [(i, target(i)) for i in range(devices)])  13.2 us
    slice x1, local copies, waits for them, and re-layouts, shards(): pieces = [blocks[a:b] for a, b in zip(edges[:-1], edges[1:])]  2.7 us
  transfers between devices with their start and end apart: 17, of which 7 were waited for; matrix products, arithmetic and copies ran while one was open for 5% of the time, Pallas kernels for 9%

profile of v1, /device:TPU:1, one launch (start us, length us, event | category | flops | bytes accessed | tf_op | source)
XLA Modules:
  0.0 93.0 jit_solution(6186697278622930240)
XLA Ops:
  0.0 0.8 compare_select_fusion
  0.8 2.1 %collective-permute-start = (s32[2,4]{1,0:T(2,128)S(1)}, s32[2,4]{1,0:T(2,128)S(1)}, u32[]{:S(2)}, u32[]{:S(2)}) collective-permute-start(s32[2,4]{1,0:T(2,128)S(1)} %compare_select_fusion), channel_id=1, source_target_pairs={{0,2},{1,3},{2,4},{3,5},{4,6},{5,7},{6,8},{7,9},{8,10},{9,11},{10,... | collective-permute-start | bytes 104 | tf_op jit(solution)/shard_map/ppermute | solution.py:125
  2.8 3.0 %collective-permute-start.1 = (s32[2,4]{1,0:T(2,128)S(1)}, s32[2,4]{1,0:T(2,128)S(1)}, u32[]{:S(2)}, u32[]{:S(2)}) collective-permute-start(s32[2,4]{1,0:T(2,128)S(1)} %compare_select_fusion), channel_id=1, source_target_pairs={{0,14},{1,15},{2,0},{3,1},{4,2},{5,3},{6,4},{7,5},{8,6},{9,7},{10,... | collective-permute-start | bytes 104 | tf_op jit(solution)/shard_map/ppermute | solution.py:125
  5.9 1.0 %collective-permute-start.16 = (bf16[8,1,2,256,256]{4,3,2,1,0:T(8,128)(2,1)}, bf16[8,1,2,256,256]{4,3,2,1,0:T(8,128)(2,1)S(1)}, u32[]{:S(2)}, u32[]{:S(2)}) collective-permute-start(bf16[8,1,2,256,256]{4,3,2,1,0:T(8,128)(2,1)} %bitcast.1), channel_id=1, source_target_pairs={{0,1},{1,0},{2,3},{3,2},{4,5},{5,4},{6,7},{7,6},{8,9},{9,8},{10,11... | collective-permute-start | bytes 6291464 | tf_op jit(solution)/shard_map/ppermute | solution.py:125
  6.8 2.7 %fusion = (bf16[2,1,2,256,256]{4,3,2,1,0:T(8,128)(2,1)}, bf16[2,1,2,256,256]{4,3,2,1,0:T(8,128)(2,1)S(1)}, bf16[2,1,2,256,256]{4,3,2,1,0:T(8,128)(2,1)}, bf16[2,1,2,256,256]{4,3,2,1,0:T(8,128)(2,1)}) fusion(bf16[8,1,2,256,256]{4,3,2,1,0:T(8,128)(2,1)} %bitcast.2), kind=kLoop, calls=%fused_computation.23 | loop fusion | bytes 4194304 | tf_op jit(solution)/shard_map/slice | solution.py:141
  9.5 1.5 %collective-permute-start.4 = (bf16[2,1,2,256,256]{4,3,2,1,0:T(8,128)(2,1)}, bf16[2,1,2,256,256]{4,3,2,1,0:T(8,128)(2,1)S(1)}, u32[]{:S(2)}, u32[]{:S(2)}) collective-permute-start(bf16[2,1,2,256,256]{4,3,2,1,0:T(8,128)(2,1)} %get-tuple-element.21), channel_id=1, source_target_pairs={{0,2},{1,3},{2,0},{3,1},{4,6},{5,7},{6,4},{7,5},{8,10},{9,11},{10,... | collective-permute-start | bytes 1572872 | tf_op jit(solution)/shard_map/ppermute | solution.py:125
  11.2 12.0 %collective-permute-done.6.refs_4_ = bf16[2,1,2,256,256]{4,3,2,1,0:T(8,128)(2,1)} collective-permute-done((bf16[2,1,2,256,256]{4,3,2,1,0:T(8,128)(2,1)S(1)}, bf16[2,1,2,256,256]{4,3,2,1,0:T(8,128)(2,1)}, u32[]{:S(2)}, u32[]{:S(2)}) %collective-permute-start.6) | collective-permute-done | bytes 524320 | tf_op jit(solution)/shard_map/ppermute | solution.py:125
  23.2 0.9 collective-permute-start.2
  24.0 1.0 %collective-permute-start.10 = (bf16[2,1,2,256,256]{4,3,2,1,0:T(8,128)(2,1)}, bf16[2,1,2,256,256]{4,3,2,1,0:T(8,128)(2,1)}, u32[]{:S(2)}, u32[]{:S(2)}) collective-permute-start(bf16[2,1,2,256,256]{4,3,2,1,0:T(8,128)(2,1)} %get-tuple-element.12), channel_id=1, source_target_pairs={{0,2},{1,3},{2,0},{3,1},{4,6},{5,7},{6,4},{7,5},{8,10},{9,11},{10,... | collective-permute-start | bytes 1572872 | tf_op jit(solution)/shard_map/ppermute | solution.py:125
  25.1 1.3 %collective-permute-start.7 = (bf16[2,1,2,256,256]{4,3,2,1,0:T(8,128)(2,1)}, bf16[2,1,2,256,256]{4,3,2,1,0:T(8,128)(2,1)S(1)}, u32[]{:S(2)}, u32[]{:S(2)}) collective-permute-start(bf16[2,1,2,256,256]{4,3,2,1,0:T(8,128)(2,1)} %collective-permute-done.6.refs_4_), channel_id=1, source_target_pairs={{0,4},{1,5},{2,14},{3,15},{4,8},{5,9},{6,2},{7,3},{8,12},{9,13},{1... | collective-permute-start | bytes 1572872 | tf_op jit(solution)/shard_map/ppermute | solution.py:125
  26.4 7.9 %collective-permute-done.4.refs_3_ = bf16[2,1,2,256,256]{4,3,2,1,0:T(8,128)(2,1)S(1)} collective-permute-done((bf16[2,1,2,256,256]{4,3,2,1,0:T(8,128)(2,1)}, bf16[2,1,2,256,256]{4,3,2,1,0:T(8,128)(2,1)S(1)}, u32[]{:S(2)}, u32[]{:S(2)}) %collective-permute-start.4) | collective-permute-done | bytes 524320 | tf_op jit(solution)/shard_map/ppermute | solution.py:125
  34.3 1.2 %collective-permute-start.3 = (s32[2,4]{1,0:T(2,128)S(1)}, s32[2,4]{1,0:T(2,128)S(1)}, u32[]{:S(2)}, u32[]{:S(2)}) collective-permute-start(s32[2,4]{1,0:T(2,128)S(1)} %compare_select_fusion), channel_id=1, source_target_pairs={{0,15},{1,0},{2,1},{3,2},{4,3},{5,4},{6,5},{7,6},{8,7},{9,8},{10,9... | collective-permute-start | bytes 104 | tf_op jit(solution)/shard_map/ppermute | solution.py:125
  35.5 10.9 %collective-permute-done.3 = s32[2,4]{1,0:T(2,128)S(1)} collective-permute-done((s32[2,4]{1,0:T(2,128)S(1)}, s32[2,4]{1,0:T(2,128)S(1)}, u32[]{:S(2)}, u32[]{:S(2)}) %collective-permute-start.3) | collective-permute-done | bytes 64 | tf_op jit(solution)/shard_map/ppermute | solution.py:125
  46.5 0.5 select_reduce_fusion.1
  47.0 0.1 copy.11
  47.1 0.1 copy.12
  47.2 0.1 reshape.30
  47.3 0.1 copy.10
  47.4 0.1 reshape.28.refs_0_
  47.5 0.1 copy.8
  47.7 0.1 copy.9
  47.9 1.0 %collective-permute-start.11 = (bf16[2,1,2,256,256]{4,3,2,1,0:T(8,128)(2,1)}, bf16[2,1,2,256,256]{4,3,2,1,0:T(8,128)(2,1)S(1)}, u32[]{:S(2)}, u32[]{:S(2)}) collective-permute-start(bf16[2,1,2,256,256]{4,3,2,1,0:T(8,128)(2,1)} %collective-permute-done.10.refs_6_), channel_id=1, source_target_pairs={{0,4},{1,5},{2,14},{3,15},{4,8},{5,9},{6,2},{7,3},{8,12},{9,13},{1... | collective-permute-start | bytes 1572872 | tf_op jit(solution)/shard_map/ppermute | solution.py:125
  49.1 7.8 %collective-permute-done.8.refs_5_ = bf16[2,1,2,256,256]{4,3,2,1,0:T(8,128)(2,1)} collective-permute-done((bf16[2,1,2,256,256]{4,3,2,1,0:T(8,128)(2,1)}, bf16[2,1,2,256,256]{4,3,2,1,0:T(8,128)(2,1)}, u32[]{:S(2)}, u32[]{:S(2)}) %collective-permute-start.8) | collective-permute-done | bytes 524320 | tf_op jit(solution)/shard_map/ppermute | solution.py:125
  56.9 4.7 %collective-permute-done.5.refs_3_ = bf16[2,1,2,256,256]{4,3,2,1,0:T(8,128)(2,1)S(1)} collective-permute-done((bf16[2,1,2,256,256]{4,3,2,1,0:T(8,128)(2,1)}, bf16[2,1,2,256,256]{4,3,2,1,0:T(8,128)(2,1)S(1)}, u32[]{:S(2)}, u32[]{:S(2)}) %collective-permute-start.5) | collective-permute-done | bytes 524320 | tf_op jit(solution)/shard_map/ppermute | solution.py:125
  61.6 0.1 broadcast_select_fusion.3
  61.7 11.1 %collective-permute-done.11.refs_6_ = bf16[2,1,2,256,256]{4,3,2,1,0:T(8,128)(2,1)S(1)} collective-permute-done((bf16[2,1,2,256,256]{4,3,2,1,0:T(8,128)(2,1)}, bf16[2,1,2,256,256]{4,3,2,1,0:T(8,128)(2,1)S(1)}, u32[]{:S(2)}, u32[]{:S(2)}) %collective-permute-start.11) | collective-permute-done | bytes 524320 | tf_op jit(solution)/shard_map/ppermute | solution.py:125
  72.8 0.1 broadcast_select_fusion
  73.0 6.0 %collective-permute-done.9.refs_5_ = bf16[2,1,2,256,256]{4,3,2,1,0:T(8,128)(2,1)S(1)} collective-permute-done((bf16[2,1,2,256,256]{4,3,2,1,0:T(8,128)(2,1)}, bf16[2,1,2,256,256]{4,3,2,1,0:T(8,128)(2,1)S(1)}, u32[]{:S(2)}, u32[]{:S(2)}) %collective-permute-start.9) | collective-permute-done | bytes 524320 | tf_op jit(solution)/shard_map/ppermute | solution.py:125
  79.0 0.1 broadcast_select_fusion.1
  79.3 5.2 %shard_map.55.refs_7_ = bf16[2,1,2,256,2560]{4,3,2,1,0:T(8,128)(2,1)} custom-call(s32[32]{0:T(128)S(1)} %pad_add_fusion.2.refs_0_, s32[4]{0:T(128)S(1)} %pad_add_fusion.3.refs_1_, bf16[2,4,1,2,256,256]{5,4,3,2,1,0:T(8,128)(2,1)S(1)} %copy-done, bf16[8,1,2,256,256]{4,3,2,1,0:T(8,128)(2,1)S(1)} %bitcast.3, ...), custom_call_target="tpu_custom_call" | custom-call | flops 2147483648 | bytes 8388608 | tf_op jit(solution)/shard_map/pallas_call | solution.py:93
  84.5 3.6 %shard_map.56.refs_11_ = bf16[2,1,2,256,2560]{4,3,2,1,0:T(8,128)(2,1)} custom-call(s32[16]{0:T(128)S(1)} %reshape.28.refs_0_, s32[2]{0:T(128)S(1)} %iota_add_fusion.2.refs_1_, bf16[2,4,1,2,256,256]{5,4,3,2,1,0:T(8,128)(2,1)S(1)} %copy-done, bf16[2,1,2,256,256]{4,3,2,1,0:T(8,128)(2,1)S(1)} %copy-done.3, ...), custom_call_target="tpu_custom_call", output_to_operand_aliasing={{}: (7, {})} | custom-call | flops 1073741824 | bytes 5242880 | tf_op jit(solution)/shard_map/pallas_call | solution.py:93
  88.1 4.9 %shard_map.57 = bf16[2,1,2,256,2560]{4,3,2,1,0:T(8,128)(2,1)} custom-call(s32[32]{0:T(128)S(1)} %pad_add_fusion.refs_0_, s32[4]{0:T(128)S(1)} %pad_add_fusion.1.refs_1_, bf16[2,4,1,2,256,256]{5,4,3,2,1,0:T(8,128)(2,1)S(1)} %copy-done, bf16[2,1,2,256,256]{4,3,2,1,0:T(8,128)(2,1)S(1)} %collective-permute-done.5.refs_3_, ...), custom_call_target="tpu_custom_call", output_to_operand_aliasing={{}: (11, {})} | custom-call | flops 2147483648 | bytes 8388608 | tf_op jit(solution)/shard_map/pallas_call | solution.py:93
  (41 shorter events, 1.0 us)
Async XLA Ops:
  0.8 23.3 %collective-permute-start = (s32[2,4]{1,0:T(2,128)S(1)}, s32[2,4]{1,0:T(2,128)S(1)}, u32[]{:S(2)}, u32[]{:S(2)}) collective-permute-start(s32[2,4]{1,0:T(2,128)S(1)} %compare_select_fusion), channel_id=1, source_target_pairs={{0,2},{1,3},{2,4},{3,5},{4,6},{5,7},{6,8},{7,9},{8,10},{9,11},{10,... | collective-permute-start | bytes 104 | tf_op jit(solution)/shard_map/ppermute | solution.py:125
  2.8 22.3 %collective-permute-start.1 = (s32[2,4]{1,0:T(2,128)S(1)}, s32[2,4]{1,0:T(2,128)S(1)}, u32[]{:S(2)}, u32[]{:S(2)}) collective-permute-start(s32[2,4]{1,0:T(2,128)S(1)} %compare_select_fusion), channel_id=1, source_target_pairs={{0,14},{1,15},{2,0},{3,1},{4,2},{5,3},{6,4},{7,5},{8,6},{9,7},{10,... | collective-permute-start | bytes 104 | tf_op jit(solution)/shard_map/ppermute | solution.py:125
  5.9 40.6 %copy-start.4 = (s32[2,4]{1,0:T(2,128)S(1)}, s32[2,4]{1,0:T(2,128)}, u32[]{:S(2)}) copy-start(s32[2,4]{1,0:T(2,128)} %param.6) | copy-start | bytes 100
  5.9 73.4 %collective-permute-start.16 = (bf16[8,1,2,256,256]{4,3,2,1,0:T(8,128)(2,1)}, bf16[8,1,2,256,256]{4,3,2,1,0:T(8,128)(2,1)S(1)}, u32[]{:S(2)}, u32[]{:S(2)}) collective-permute-start(bf16[8,1,2,256,256]{4,3,2,1,0:T(8,128)(2,1)} %bitcast.1), channel_id=1, source_target_pairs={{0,1},{1,0},{2,3},{3,2},{4,5},{5,4},{6,7},{7,6},{8,9},{9,8},{10,11... | collective-permute-start | bytes 6291464 | tf_op jit(solution)/shard_map/ppermute | solution.py:125
  9.5 13.7 %collective-permute-start.6 = (bf16[2,1,2,256,256]{4,3,2,1,0:T(8,128)(2,1)S(1)}, bf16[2,1,2,256,256]{4,3,2,1,0:T(8,128)(2,1)}, u32[]{:S(2)}, u32[]{:S(2)}) collective-permute-start(bf16[2,1,2,256,256]{4,3,2,1,0:T(8,128)(2,1)S(1)} %get-tuple-element.19), channel_id=1, source_target_pairs={{0,2},{1,3},{2,0},{3,1},{4,6},{5,7},{6,4},{7,5},{8,10},{9,11},{10,... | collective-permute-start | bytes 1572872 | tf_op jit(solution)/shard_map/ppermute | solution.py:125
  9.5 24.8 %collective-permute-start.4 = (bf16[2,1,2,256,256]{4,3,2,1,0:T(8,128)(2,1)}, bf16[2,1,2,256,256]{4,3,2,1,0:T(8,128)(2,1)S(1)}, u32[]{:S(2)}, u32[]{:S(2)}) collective-permute-start(bf16[2,1,2,256,256]{4,3,2,1,0:T(8,128)(2,1)} %get-tuple-element.21), channel_id=1, source_target_pairs={{0,2},{1,3},{2,0},{3,1},{4,6},{5,7},{6,4},{7,5},{8,10},{9,11},{10,... | collective-permute-start | bytes 1572872 | tf_op jit(solution)/shard_map/ppermute | solution.py:125
  23.2 12.3 %collective-permute-start.2 = (s32[2,4]{1,0:T(2,128)S(1)}, s32[2,4]{1,0:T(2,128)S(1)}, u32[]{:S(2)}, u32[]{:S(2)}) collective-permute-start(s32[2,4]{1,0:T(2,128)S(1)} %compare_select_fusion), channel_id=1, source_target_pairs={{0,1},{1,2},{2,3},{3,4},{4,5},{5,6},{6,7},{7,8},{8,9},{9,10},{10,1... | collective-permute-start | bytes 104 | tf_op jit(solution)/shard_map/ppermute | solution.py:125
  24.0 23.9 %collective-permute-start.10 = (bf16[2,1,2,256,256]{4,3,2,1,0:T(8,128)(2,1)}, bf16[2,1,2,256,256]{4,3,2,1,0:T(8,128)(2,1)}, u32[]{:S(2)}, u32[]{:S(2)}) collective-permute-start(bf16[2,1,2,256,256]{4,3,2,1,0:T(8,128)(2,1)} %get-tuple-element.12), channel_id=1, source_target_pairs={{0,2},{1,3},{2,0},{3,1},{4,6},{5,7},{6,4},{7,5},{8,10},{9,11},{10,... | collective-permute-start | bytes 1572872 | tf_op jit(solution)/shard_map/ppermute | solution.py:125
  25.1 23.8 %collective-permute-start.7 = (bf16[2,1,2,256,256]{4,3,2,1,0:T(8,128)(2,1)}, bf16[2,1,2,256,256]{4,3,2,1,0:T(8,128)(2,1)S(1)}, u32[]{:S(2)}, u32[]{:S(2)}) collective-permute-start(bf16[2,1,2,256,256]{4,3,2,1,0:T(8,128)(2,1)} %collective-permute-done.6.refs_4_), channel_id=1, source_target_pairs={{0,4},{1,5},{2,14},{3,15},{4,8},{5,9},{6,2},{7,3},{8,12},{9,13},{1... | collective-permute-start | bytes 1572872 | tf_op jit(solution)/shard_map/ppermute | solution.py:125
  34.3 1.2 %copy-start.2 = (bf16[2,1,2,256,256]{4,3,2,1,0:T(8,128)(2,1)}, bf16[2,1,2,256,256]{4,3,2,1,0:T(8,128)(2,1)S(1)}, u32[]{:S(2)}) copy-start(bf16[2,1,2,256,256]{4,3,2,1,0:T(8,128)(2,1)S(1)} %collective-permute-done.4.refs_3_) | copy-start | bytes 1572868
  34.3 12.1 %collective-permute-start.3 = (s32[2,4]{1,0:T(2,128)S(1)}, s32[2,4]{1,0:T(2,128)S(1)}, u32[]{:S(2)}, u32[]{:S(2)}) collective-permute-start(s32[2,4]{1,0:T(2,128)S(1)} %compare_select_fusion), channel_id=1, source_target_pairs={{0,15},{1,0},{2,1},{3,2},{4,3},{5,4},{6,5},{7,6},{8,7},{9,8},{10,9... | collective-permute-start | bytes 104 | tf_op jit(solution)/shard_map/ppermute | solution.py:125
  35.5 21.4 %collective-permute-start.8 = (bf16[2,1,2,256,256]{4,3,2,1,0:T(8,128)(2,1)}, bf16[2,1,2,256,256]{4,3,2,1,0:T(8,128)(2,1)}, u32[]{:S(2)}, u32[]{:S(2)}) collective-permute-start(bf16[2,1,2,256,256]{4,3,2,1,0:T(8,128)(2,1)} %get-tuple-element.11), channel_id=1, source_target_pairs={{0,2},{1,3},{2,0},{3,1},{4,6},{5,7},{6,4},{7,5},{8,10},{9,11},{10,... | collective-permute-start | bytes 1572872 | tf_op jit(solution)/shard_map/ppermute | solution.py:125
  46.4 15.1 %collective-permute-start.5 = (bf16[2,1,2,256,256]{4,3,2,1,0:T(8,128)(2,1)}, bf16[2,1,2,256,256]{4,3,2,1,0:T(8,128)(2,1)S(1)}, u32[]{:S(2)}, u32[]{:S(2)}) collective-permute-start(bf16[2,1,2,256,256]{4,3,2,1,0:T(8,128)(2,1)} %copy-done.2), channel_id=1, source_target_pairs={{0,4},{1,5},{2,14},{3,15},{4,8},{5,9},{6,2},{7,3},{8,12},{9,13},{1... | collective-permute-start | bytes 1572872 | tf_op jit(solution)/shard_map/ppermute | solution.py:125
  47.9 24.9 %collective-permute-start.11 = (bf16[2,1,2,256,256]{4,3,2,1,0:T(8,128)(2,1)}, bf16[2,1,2,256,256]{4,3,2,1,0:T(8,128)(2,1)S(1)}, u32[]{:S(2)}, u32[]{:S(2)}) collective-permute-start(bf16[2,1,2,256,256]{4,3,2,1,0:T(8,128)(2,1)} %collective-permute-done.10.refs_6_), channel_id=1, source_target_pairs={{0,4},{1,5},{2,14},{3,15},{4,8},{5,9},{6,2},{7,3},{8,12},{9,13},{1... | collective-permute-start | bytes 1572872 | tf_op jit(solution)/shard_map/ppermute | solution.py:125
  49.0 30.3 %copy-start = (bf16[2,4,1,2,256,256]{5,4,3,2,1,0:T(8,128)(2,1)S(1)}, bf16[2,4,1,2,256,256]{5,4,3,2,1,0:T(8,128)(2,1)}, u32[]{:S(2)}) copy-start(bf16[2,4,1,2,256,256]{5,4,3,2,1,0:T(8,128)(2,1)} %refs_2_.5) | copy-start | bytes 6291460
  49.0 30.3 %copy-start.1 = (bf16[2,4,1,2,256,256]{5,4,3,2,1,0:T(8,128)(2,1)S(1)}, bf16[2,4,1,2,256,256]{5,4,3,2,1,0:T(8,128)(2,1)}, u32[]{:S(2)}) copy-start(bf16[2,4,1,2,256,256]{5,4,3,2,1,0:T(8,128)(2,1)} %param.7) | copy-start | bytes 6291460
  49.0 39.1 %collective-permute-start.13 = (bf16[2,1,2,256,256]{4,3,2,1,0:T(8,128)(2,1)S(1)}, bf16[2,1,2,256,256]{4,3,2,1,0:T(8,128)(2,1)S(1)}, u32[]{:S(2)}, u32[]{:S(2)}) collective-permute-start(bf16[2,1,2,256,256]{4,3,2,1,0:T(8,128)(2,1)S(1)} %broadcast_select_fusion.2), channel_id=1, source_target_pairs={{0,1},{1,0},{2,3},{3,2},{4,5},{5,4},{6,7},{7,6},{8,9},{9,8},{10,11... | collective-permute-start | bytes 1572872 | tf_op jit(solution)/shard_map/ppermute | solution.py:125
  56.9 22.1 %collective-permute-start.9 = (bf16[2,1,2,256,256]{4,3,2,1,0:T(8,128)(2,1)}, bf16[2,1,2,256,256]{4,3,2,1,0:T(8,128)(2,1)S(1)}, u32[]{:S(2)}, u32[]{:S(2)}) collective-permute-start(bf16[2,1,2,256,256]{4,3,2,1,0:T(8,128)(2,1)} %collective-permute-done.8.refs_5_), channel_id=1, source_target_pairs={{0,4},{1,5},{2,14},{3,15},{4,8},{5,9},{6,2},{7,3},{8,12},{9,13},{1... | collective-permute-start | bytes 1572872 | tf_op jit(solution)/shard_map/ppermute | solution.py:125
  61.6 26.5 %collective-permute-start.12 = (bf16[2,1,2,256,256]{4,3,2,1,0:T(8,128)(2,1)S(1)}, bf16[2,1,2,256,256]{4,3,2,1,0:T(8,128)(2,1)S(1)}, u32[]{:S(2)}, u32[]{:S(2)}) collective-permute-start(bf16[2,1,2,256,256]{4,3,2,1,0:T(8,128)(2,1)S(1)} %broadcast_select_fusion.3), channel_id=1, source_target_pairs={{0,1},{1,0},{2,3},{3,2},{4,5},{5,4},{6,7},{7,6},{8,9},{9,8},{10,11... | collective-permute-start | bytes 1572872 | tf_op jit(solution)/shard_map/ppermute | solution.py:125
  72.9 15.2 %collective-permute-start.15 = (bf16[2,1,2,256,256]{4,3,2,1,0:T(8,128)(2,1)S(1)}, bf16[2,1,2,256,256]{4,3,2,1,0:T(8,128)(2,1)S(1)}, u32[]{:S(2)}, u32[]{:S(2)}) collective-permute-start(bf16[2,1,2,256,256]{4,3,2,1,0:T(8,128)(2,1)S(1)} %broadcast_select_fusion), channel_id=1, source_target_pairs={{0,1},{1,0},{2,3},{3,2},{4,5},{5,4},{6,7},{7,6},{8,9},{9,8},{10,11... | collective-permute-start | bytes 1572872 | tf_op jit(solution)/shard_map/ppermute | solution.py:125
  79.0 9.1 %collective-permute-start.14 = (bf16[2,1,2,256,256]{4,3,2,1,0:T(8,128)(2,1)S(1)}, bf16[2,1,2,256,256]{4,3,2,1,0:T(8,128)(2,1)S(1)}, u32[]{:S(2)}, u32[]{:S(2)}) collective-permute-start(bf16[2,1,2,256,256]{4,3,2,1,0:T(8,128)(2,1)S(1)} %broadcast_select_fusion.1), channel_id=1, source_target_pairs={{0,1},{1,0},{2,3},{3,2},{4,5},{5,4},{6,7},{7,6},{8,9},{9,8},{10,11... | collective-permute-start | bytes 1572872 | tf_op jit(solution)/shard_map/ppermute | solution.py:125
  79.3 5.2 %copy-start.3 = (bf16[2,1,2,256,256]{4,3,2,1,0:T(8,128)(2,1)S(1)}, bf16[2,1,2,256,256]{4,3,2,1,0:T(8,128)(2,1)}, u32[]{:S(2)}) copy-start(bf16[2,1,2,256,256]{4,3,2,1,0:T(8,128)(2,1)} %copy-done.2) | copy-start | bytes 1572868

commit v2 on v1

--- a/solution.py
+++ b/solution.py
@@ -8,7 +8,11 @@
 from jax.sharding import PartitionSpec as P
 
 HALF = 2
+VMEM_BYTES = 16 * 2**20
 CHUNKS = (2, 2, 2, 2)
+CARRIER = 1
+LIST_ROWS = 16
+BASE = 128
 
 
 def product_kernel(groups, arrays, slots, aliased, *refs):
@@ -18,7 +22,9 @@
     out_ref, slab_v, block_v, total, out_v, slab_sem, block_sem, out_sem = refs
     rows, _, freqs = slab_ref.shape[:3]
     side = slab_ref.shape[4]
-    sources = [ref.at[i] for ref in chunk_refs for i in range(ref.shape[0])]
+    sources = [
+        ref.at[i, :, :, pl.ds(0, side)] for ref in chunk_refs for i in range(ref.shape[0])
+    ]
 
     def needed(b):
         hit = match_ref[b * rows] >= 0
@@ -105,7 +111,7 @@
             pltpu.SemaphoreType.DMA((groups, rows)),
         ],
         input_output_aliases={} if before is None else {len(operands) - 1: 0},
-        compiler_params=pltpu.CompilerParams(vmem_limit_bytes=32 * 2**20),
+        compiler_params=pltpu.CompilerParams(vmem_limit_bytes=VMEM_BYTES),
         cost_estimate=pl.CostEstimate(
             flops=groups * slots * rows * 4 * freqs * side**3,
             bytes_accessed=2 * (slab.size + groups * (slots + rows) * freqs * parts * side * side),
@@ -114,6 +120,24 @@
     )(*operands)
 
 
+def after(value, *others):
+    return lax.optimization_barrier((value, *others))
+
+
+def with_list(block, entries):
+    flat = entries.reshape(-1) + BASE
+    coded = jnp.stack([flat // BASE, flat % BASE]).astype(block.dtype)
+    below = jnp.zeros(block.shape[:-2] + (LIST_ROWS, block.shape[-1]), block.dtype)
+    below = lax.dynamic_update_slice(below, coded[None, None, None], (0,) * below.ndim)
+    return jnp.concatenate([block, below], axis=-2)
+
+
+def list_of(block, shape):
+    count = shape[0] * shape[1]
+    coded = block[0, 0, 0, -LIST_ROWS : -LIST_ROWS + 2, :count].astype(jnp.int32)
+    return (coded[0] * BASE + coded[1] - BASE).reshape(shape)
+
+
 def shards(slab, slab_cols, panels, panel_rows, panel_live):
     rows, _, freqs, parts, side, _ = slab.shape
     cols, slots = panel_rows.shape
@@ -137,25 +161,20 @@
     own_rows = jnp.where(live, panel_rows, -1)
 
     blocks = panels.reshape((cols * slots,) + panels.shape[2:])
-    edges = [sum(CHUNKS[:k]) for k in range(len(CHUNKS) + 1)]
-    pieces = [blocks[a:b] for a, b in zip(edges[:-1], edges[1:])]
-    across, along, passed = [], [], []
+    count = len(CHUNKS)
+    edges = [sum(CHUNKS[:k]) for k in range(count + 1)]
+
+    def cut(source, k):
+        return source[edges[k] : edges[k + 1]]
+
     sends_across = core == odd
 
-    for k in range(len(pieces)):
-        if k >= 2:
-            across[k - 2], pieces[k] = lax.optimization_barrier((across[k - 2], pieces[k]))
-        across.append(permuted(pieces[k], partner_chip))
-    swapped = permuted(blocks, partner_core)
-    for k in range(len(pieces)):
-        along.append(permuted(across[k], onward))
-    for k in range(len(pieces)):
-        handed = jnp.where(sends_across, across[k], along[k])
-        passed.append(permuted(handed, partner_core))
-
-    rows_of = {0: own_rows}
-    for s in (1, -1, 2, -2):
-        rows_of[s] = permuted(own_rows, lambda i, s=s: (i - s) % devices)
+    def hand_over(first, last):
+        handed = [
+            jnp.where(sends_across, across[k][..., :side, :], along[k][..., :side, :])
+            for k in range(first, last)
+        ]
+        return permuted(jnp.concatenate(handed), partner_core)
 
     def matches(s, g_rows):
         same = g_rows[:, :, None, None] == slab_cols[None, None, :, :]
@@ -173,18 +192,33 @@
         chunks = [c for _, _, cs in sources for c in cs]
         return products(slab, match, place, chunks, out_shape, before)
 
-    side_near = jnp.where(core == 0, 1, -1)
-    rows_near = jnp.where(core == 0, rows_of[1], rows_of[-1])
-    rows_far = jnp.where(core == 0, rows_of[-1], rows_of[1])
-    side_across = jnp.where(odd == 0, 2, -2)
-    rows_across = jnp.where(odd == 0, rows_of[2], rows_of[-2])
-    rows_along = jnp.where(odd == 0, rows_of[-2], rows_of[2])
-
-    out = step([(0, own_rows, [blocks]), (side_near, rows_near, [swapped])], None)
-    out = step([(side_across, rows_across, across)], out)
-    out = step([(-side_across, rows_along, along), (-side_near, rows_far, passed)], out)
-    return out
-
+    near = jnp.where(core == 0, 1, -1)
+    over = jnp.where(odd == 0, 2, -2)
+
+    piece = cut(blocks, 0)
+    rest, piece = after(blocks, piece)
+    pieces = [piece] + [cut(rest, k) for k in range(1, count)]
+    pieces[CARRIER] = with_list(pieces[CARRIER], own_rows)
+    across, along, passed = [], [], []
+    for k in range(count):
+        if k >= 2:
+            across[k - 2], pieces[k] = after(across[k - 2], pieces[k])
+        across.append(permuted(pieces[k], partner_chip))
+    rows_across = list_of(across[CARRIER], own_rows.shape)
+    whole, listed, across[1] = after(blocks, own_rows, across[1])
+    swapped = permuted(whole, partner_core)
+    rows_near = permuted(listed, partner_core)
+    out = step([(0, own_rows, [blocks]), (near, rows_near, [swapped])], None)
+    along.append(permuted(across[0], onward))
+    along.append(permuted(across[1], onward))
+    along.append(permuted(across[2], onward))
+    along.append(permuted(across[3], onward))
+    rows_along = list_of(along[CARRIER], own_rows.shape)
+    rows_far = permuted(jnp.where(sends_across, rows_across, rows_along), partner_core)
+    along[3], out = after(along[3], out)
+    passed = [hand_over(0, 2), hand_over(2, 3), hand_over(3, 4)]
+    out = step([(over, rows_across, across)], out)
+    return step([(-over, rows_along, along), (-near, rows_far, passed)], out)
 
 def solution(mesh):
     placed = (

time: 92.9 us -> 82.3 us (0.89)
  waiting for transfers between devices: 60.5 us -> 32.7 us
  starting transfers between devices: 13.2 us -> 20.2 us
  other arithmetic: 1.9 us -> 8.02 us
  local copies, waits for them, and re-layouts: 3.64 us -> 5.8 us
  Pallas kernels: 13.7 us -> 14.8 us
    ppermute x17 -> x14, waiting for transfers between devices: 60.5 us -> 32.7 us  [permuted(): return lax.ppermute(value, 'blk', [(i, target(i)) for i in range(devices)])]
    ppermute x17 -> x14, starting transfers between devices: 13.2 us -> 20.2 us  [permuted(): return lax.ppermute(value, 'blk', [(i, target(i)) for i in range(devices)])]
    select_n x7 -> x5, other arithmetic: 1.08 us -> 4.73 us  [the longest x4 4.73 us: hand_over(): jnp.where(sends_across, across[k][..., :side, :], along[k][..., :side, :])]
    concatenate x0 -> x2, other arithmetic: none -> 2.31 us  [the longest x1 2.27 us: hand_over(): return permuted(jnp.concatenate(handed), partner_core)]
    pallas_call x3, Pallas kernels: 13.7 us -> 14.8 us  [products(): pl.pallas_call(functools.partial(product_kernel, groups, len(chunks), slo...]
    unnamed x10 -> x16, local copies, waits for them, and re-layouts: 0.02 us -> 1.08 us
    slice x1 -> x2, local copies, waits for them, and re-layouts: 2.7 us -> 3.55 us  [cut(): return source[edges[k]:edges[k + 1]]]
  transfers between devices with their start and end apart: 17 -> 14, of which waited for: 7 -> 6; matrix products, arithmetic and copies ran while one was open for 5% -> 14% of each run, Pallas kernels for 9% -> 12%
where the time goes in v2:
time: 82.3 us; the launch traced here: 81.6 us
  waiting for transfers between devices  32.7 us (40%)
  starting transfers between devices  20.2 us (25%)
  Pallas kernels  14.8 us (18%)
  other arithmetic  8.02 us (10%)
  local copies, waits for them, and re-layouts  5.8 us (7%)
    ppermute x14, waiting for transfers between devices, permuted(): return lax.ppermute(value, 'blk', [(i, target(i)) for i in range(devices)])  32.7 us
    ppermute x14, starting transfers between devices, permuted(): return lax.ppermute(value, 'blk', [(i, target(i)) for i in range(devices)])  20.2 us
    pallas_call x3, Pallas kernels, products(): pl.pallas_call(functools.partial(product_kernel, groups, len(chunks), slo...  14.8 us
    select_n x4, other arithmetic, hand_over(): jnp.where(sends_across, across[k][..., :side, :], along[k][..., :side, :])  4.73 us
    slice x2, local copies, waits for them, and re-layouts, cut(): return source[edges[k]:edges[k + 1]]  3.55 us
    concatenate x1, other arithmetic, hand_over(): return permuted(jnp.concatenate(handed), partner_core)  2.27 us
  transfers between devices with their start and end apart: 14, of which 6 were waited for; matrix products, arithmetic and copies ran while one was open for 14% of the time, Pallas kernels for 12%

profile of v2, /device:TPU:1, one launch (start us, length us, event | category | flops | bytes accessed | tf_op | source)
XLA Modules:
  0.0 81.6 jit_solution(9590719891624667026)
XLA Ops:
  0.0 1.1 %slice.52 = bf16[2,1,2,256,256]{4,3,2,1,0:T(8,128)(2,1)S(1)} slice(bf16[8,1,2,256,256]{4,3,2,1,0:T(8,128)(2,1)} %bitcast.refs_3_), slice={[0:2], [0:1], [0:2], [0:256], [0:256]} | slice | bytes 1048576 | tf_op jit(solution)/shard_map/slice | solution.py:168
  1.1 2.1 %collective-permute-start.3 = (bf16[2,1,2,256,256]{4,3,2,1,0:T(8,128)(2,1)S(1)}, bf16[2,1,2,256,256]{4,3,2,1,0:T(8,128)(2,1)S(1)}, u32[]{:S(2)}, u32[]{:S(2)}) collective-permute-start(bf16[2,1,2,256,256]{4,3,2,1,0:T(8,128)(2,1)S(1)} %slice.52), channel_id=1, source_target_pairs={{0,2},{1,3},{2,0},{3,1},{4,6},{5,7},{6,4},{7,5},{8,10},{9,11},{10,... | collective-permute-start | bytes 1572872 | tf_op jit(solution)/shard_map/ppermute | solution.py:149
  3.2 2.4 %fusion.14 = (bf16[2,1,2,256,256]{4,3,2,1,0:T(8,128)(2,1)}, bf16[2,1,2,256,256]{4,3,2,1,0:T(8,128)(2,1)}, bf16[2,1,2,256,256]{4,3,2,1,0:T(8,128)(2,1)S(1)}) fusion(bf16[8,1,2,256,256]{4,3,2,1,0:T(8,128)(2,1)} %bitcast.refs_3_), kind=kLoop, calls=%fused_computation.51 | loop fusion | bytes 3145728 | tf_op jit(solution)/shard_map/slice | solution.py:168
  6.0 8.9 %collective-permute-done.3.refs_3_ = bf16[2,1,2,256,256]{4,3,2,1,0:T(8,128)(2,1)S(1)} collective-permute-done((bf16[2,1,2,256,256]{4,3,2,1,0:T(8,128)(2,1)S(1)}, bf16[2,1,2,256,256]{4,3,2,1,0:T(8,128)(2,1)S(1)}, u32[]{:S(2)}, u32[]{:S(2)}) %collective-permute-start.3) | collective-permute-done | bytes 524320 | tf_op jit(solution)/shard_map/ppermute | solution.py:149
  14.9 1.1 %collective-permute-start.5 = (bf16[2,1,2,256,256]{4,3,2,1,0:T(8,128)(2,1)}, bf16[2,1,2,256,256]{4,3,2,1,0:T(8,128)(2,1)}, u32[]{:S(2)}, u32[]{:S(2)}) collective-permute-start(bf16[2,1,2,256,256]{4,3,2,1,0:T(8,128)(2,1)} %get-tuple-element.21), channel_id=1, source_target_pairs={{0,2},{1,3},{2,0},{3,1},{4,6},{5,7},{6,4},{7,5},{8,10},{9,11},{10,... | collective-permute-start | bytes 1572872 | tf_op jit(solution)/shard_map/ppermute | solution.py:149
  16.0 1.3 %collective-permute-start.4 = (bf16[2,1,2,256,256]{4,3,2,1,0:T(8,128)(2,1)S(1)}, bf16[2,1,2,256,256]{4,3,2,1,0:T(8,128)(2,1)S(1)}, u32[]{:S(2)}, u32[]{:S(2)}) collective-permute-start(bf16[2,1,2,256,256]{4,3,2,1,0:T(8,128)(2,1)S(1)} %collective-permute-done.3.refs_3_), channel_id=1, source_target_pairs={{0,4},{1,5},{2,14},{3,15},{4,8},{5,9},{6,2},{7,3},{8,12},{9,13},{1... | collective-permute-start | bytes 1572872 | tf_op jit(solution)/shard_map/ppermute | solution.py:149
  17.3 9.5 %collective-permute-done.refs_4_ = bf16[2,1,2,272,256]{4,3,2,1,0:T(8,128)(2,1)S(1)} collective-permute-done((bf16[2,1,2,272,256]{4,3,2,1,0:T(8,128)(2,1)S(1)}, bf16[2,1,2,272,256]{4,3,2,1,0:T(8,128)(2,1)S(1)}, u32[]{:S(2)}, u32[]{:S(2)}) %collective-permute-start) | collective-permute-done | bytes 557088 | tf_op jit(solution)/shard_map/ppermute | solution.py:149
  26.8 2.1 %collective-permute-start.10 = (bf16[8,1,2,256,256]{4,3,2,1,0:T(8,128)(2,1)}, bf16[8,1,2,256,256]{4,3,2,1,0:T(8,128)(2,1)}, u32[]{:S(2)}, u32[]{:S(2)}) collective-permute-start(bf16[8,1,2,256,256]{4,3,2,1,0:T(8,128)(2,1)} %bitcast.refs_3_), channel_id=1, source_target_pairs={{0,1},{1,0},{2,3},{3,2},{4,5},{5,4},{6,7},{7,6},{8,9},{9,8},{10,11... | collective-permute-start | bytes 6291464 | tf_op jit(solution)/shard_map/ppermute | solution.py:149
  29.0 1.8 %collective-permute-start.1 = (bf16[2,1,2,272,256]{4,3,2,1,0:T(8,128)(2,1)S(1)}, bf16[2,1,2,272,256]{4,3,2,1,0:T(8,128)(2,1)S(1)}, u32[]{:S(2)}, u32[]{:S(2)}) collective-permute-start(bf16[2,1,2,272,256]{4,3,2,1,0:T(8,128)(2,1)S(1)} %collective-permute-done.refs_4_), channel_id=1, source_target_pairs={{0,4},{1,5},{2,14},{3,15},{4,8},{5,9},{6,2},{7,3},{8,12},{9,13},{1... | collective-permute-start | bytes 1671176 | tf_op jit(solution)/shard_map/ppermute | solution.py:149
  30.8 3.3 %collective-permute-start.7 = (bf16[2,1,2,256,256]{4,3,2,1,0:T(8,128)(2,1)}, bf16[2,1,2,256,256]{4,3,2,1,0:T(8,128)(2,1)}, u32[]{:S(2)}, u32[]{:S(2)}) collective-permute-start(bf16[2,1,2,256,256]{4,3,2,1,0:T(8,128)(2,1)} %get-tuple-element.22), channel_id=1, source_target_pairs={{0,2},{1,3},{2,0},{3,1},{4,6},{5,7},{6,4},{7,5},{8,10},{9,11},{10,... | collective-permute-start | bytes 1572872 | tf_op jit(solution)/shard_map/ppermute | solution.py:149
  34.2 4.0 %collective-permute-done.5.refs_5_ = bf16[2,1,2,256,256]{4,3,2,1,0:T(8,128)(2,1)} collective-permute-done((bf16[2,1,2,256,256]{4,3,2,1,0:T(8,128)(2,1)}, bf16[2,1,2,256,256]{4,3,2,1,0:T(8,128)(2,1)}, u32[]{:S(2)}, u32[]{:S(2)}) %collective-permute-start.5) | collective-permute-done | bytes 524320 | tf_op jit(solution)/shard_map/ppermute | solution.py:149
  38.2 2.1 %collective-permute-start.9 = (s32[2,4]{1,0:T(2,128)S(1)}, s32[2,4]{1,0:T(2,128)S(1)}, u32[]{:S(2)}, u32[]{:S(2)}) collective-permute-start(s32[2,4]{1,0:T(2,128)S(1)} %get-tuple-element.23), channel_id=1, source_target_pairs={{0,1},{1,0},{2,3},{3,2},{4,5},{5,4},{6,7},{7,6},{8,9},{9,8},{10,11... | collective-permute-start | bytes 104 | tf_op jit(solution)/shard_map/ppermute | solution.py:149
  40.2 1.8 %collective-permute-start.6 = (bf16[2,1,2,256,256]{4,3,2,1,0:T(8,128)(2,1)}, bf16[2,1,2,256,256]{4,3,2,1,0:T(8,128)(2,1)}, u32[]{:S(2)}, u32[]{:S(2)}) collective-permute-start(bf16[2,1,2,256,256]{4,3,2,1,0:T(8,128)(2,1)} %collective-permute-done.5.refs_5_), channel_id=1, source_target_pairs={{0,4},{1,5},{2,14},{3,15},{4,8},{5,9},{6,2},{7,3},{8,12},{9,13},{1... | collective-permute-start | bytes 1572872 | tf_op jit(solution)/shard_map/ppermute | solution.py:149
  42.1 0.8 %broadcast_select_fusion.2 = bf16[2,1,2,256,256]{4,3,2,1,0:T(8,128)(2,1)} fusion(bf16[2,1,2,256,256]{4,3,2,1,0:T(8,128)(2,1)S(1)} %collective-permute-done.3.refs_3_, bf16[2,1,2,256,256]{4,3,2,1,0:T(8,128)(2,1)S(1)} %collective-permute-done.4.refs_3_, pred[]{:T(512)S(6)} %eq.36), kind=kLoop, calls=%fused_computation.5 | loop fusion | flops 262144 | bytes 1572865 | tf_op jit(solution)/shard_map/jit(_where)/select_n | solution.py:174
  42.9 6.5 %collective-permute-done.7.refs_6_ = bf16[2,1,2,256,256]{4,3,2,1,0:T(8,128)(2,1)} collective-permute-done((bf16[2,1,2,256,256]{4,3,2,1,0:T(8,128)(2,1)}, bf16[2,1,2,256,256]{4,3,2,1,0:T(8,128)(2,1)}, u32[]{:S(2)}, u32[]{:S(2)}) %collective-permute-start.7) | collective-permute-done | bytes 524320 | tf_op jit(solution)/shard_map/ppermute | solution.py:149
  49.4 1.2 %collective-permute-start.8 = (bf16[2,1,2,256,256]{4,3,2,1,0:T(8,128)(2,1)}, bf16[2,1,2,256,256]{4,3,2,1,0:T(8,128)(2,1)}, u32[]{:S(2)}, u32[]{:S(2)}) collective-permute-start(bf16[2,1,2,256,256]{4,3,2,1,0:T(8,128)(2,1)} %collective-permute-done.7.refs_6_), channel_id=1, source_target_pairs={{0,4},{1,5},{2,14},{3,15},{4,8},{5,9},{6,2},{7,3},{8,12},{9,13},{1... | collective-permute-start | bytes 1572872 | tf_op jit(solution)/shard_map/ppermute | solution.py:149
  50.7 1.8 %collective-permute-start.2 = (s32[2,4]{1,0:T(2,128)S(1)}, s32[2,4]{1,0:T(2,128)S(1)}, u32[]{:S(2)}, u32[]{:S(2)}) collective-permute-start(s32[2,4]{1,0:T(2,128)S(1)} %broadcast_select_fusion.3), channel_id=1, source_target_pairs={{0,1},{1,0},{2,3},{3,2},{4,5},{5,4},{6,7},{7,6},{8,9},{9,8},{10,11... | collective-permute-start | bytes 104 | tf_op jit(solution)/shard_map/ppermute | solution.py:149
  52.6 2.3 %pad_maximum_fusion = bf16[4,1,2,256,256]{4,3,2,1,0:T(8,128)(2,1)} fusion(bf16[2,1,2,256,256]{4,3,2,1,0:T(8,128)(2,1)S(1)} %slice_select_fusion, bf16[2,1,2,256,256]{4,3,2,1,0:T(8,128)(2,1)} %broadcast_select_fusion.2), kind=kLoop, calls=%fused_computation | loop fusion | flops 524288 | bytes 2097152 | tf_op jit(solution)/shard_map/concatenate | solution.py:177
  54.9 0.5 select_reduce_fusion
  55.4 0.1 copy.10
  55.6 0.1 copy.11
  55.9 1.2 %collective-permute-done.6.refs_5_ = bf16[2,1,2,256,256]{4,3,2,1,0:T(8,128)(2,1)} collective-permute-done((bf16[2,1,2,256,256]{4,3,2,1,0:T(8,128)(2,1)}, bf16[2,1,2,256,256]{4,3,2,1,0:T(8,128)(2,1)}, u32[]{:S(2)}, u32[]{:S(2)}) %collective-permute-start.6) | collective-permute-done | bytes 524320 | tf_op jit(solution)/shard_map/ppermute | solution.py:149
  57.1 1.9 %broadcast_select_fusion.1 = bf16[2,1,2,256,256]{4,3,2,1,0:T(8,128)(2,1)} fusion(bf16[2,1,2,256,256]{4,3,2,1,0:T(8,128)(2,1)} %collective-permute-done.5.refs_5_, bf16[2,1,2,256,256]{4,3,2,1,0:T(8,128)(2,1)} %collective-permute-done.6.refs_5_, pred[]{:T(512)S(6)} %eq.36), kind=kLoop, calls=%fused_computation.4 | loop fusion | flops 262144 | bytes 1572865 | tf_op jit(solution)/shard_map/jit(_where)/select_n | solution.py:174
  59.1 0.8 %collective-permute-start.12 = (bf16[2,1,2,256,256]{4,3,2,1,0:T(8,128)(2,1)}, bf16[2,1,2,256,256]{4,3,2,1,0:T(8,128)(2,1)}, u32[]{:S(2)}, u32[]{:S(2)}) collective-permute-start(bf16[2,1,2,256,256]{4,3,2,1,0:T(8,128)(2,1)} %broadcast_select_fusion.1), channel_id=1, source_target_pairs={{0,1},{1,0},{2,3},{3,2},{4,5},{5,4},{6,7},{7,6},{8,9},{9,8},{10,11... | collective-permute-start | bytes 1572872 | tf_op jit(solution)/shard_map/ppermute | solution.py:149
  59.9 5.8 %shard_map.55.refs_7_ = bf16[2,1,2,256,2560]{4,3,2,1,0:T(8,128)(2,1)} custom-call(s32[32]{0:T(128)S(1)} %pad_add_fusion.2.refs_0_, s32[4]{0:T(128)S(1)} %pad_add_fusion.3.refs_1_, bf16[2,4,1,2,256,256]{5,4,3,2,1,0:T(8,128)(2,1)S(1)} %copy-done, bf16[8,1,2,256,256]{4,3,2,1,0:T(8,128)(2,1)} %bitcast.refs_3_, ...), custom_call_target="tpu_custom_call" | custom-call | flops 2147483648 | bytes 8388608 | tf_op jit(solution)/shard_map/pallas_call | solution.py:99
  65.8 2.6 %collective-permute-done.8.refs_6_ = bf16[2,1,2,256,256]{4,3,2,1,0:T(8,128)(2,1)} collective-permute-done((bf16[2,1,2,256,256]{4,3,2,1,0:T(8,128)(2,1)}, bf16[2,1,2,256,256]{4,3,2,1,0:T(8,128)(2,1)}, u32[]{:S(2)}, u32[]{:S(2)}) %collective-permute-start.8) | collective-permute-done | bytes 524320 | tf_op jit(solution)/shard_map/ppermute | solution.py:149
  68.4 1.9 %broadcast_select_fusion = bf16[2,1,2,256,256]{4,3,2,1,0:T(8,128)(2,1)} fusion(bf16[2,1,2,256,256]{4,3,2,1,0:T(8,128)(2,1)} %collective-permute-done.7.refs_6_, bf16[2,1,2,256,256]{4,3,2,1,0:T(8,128)(2,1)} %collective-permute-done.8.refs_6_, pred[]{:T(512)S(6)} %eq.36), kind=kLoop, calls=%fused_computation.3 | loop fusion | flops 262144 | bytes 1572865 | tf_op jit(solution)/shard_map/jit(_where)/select_n | solution.py:174
  70.3 0.6 collective-permute-start.13
  71.1 0.1 copy.8
  71.6 1.1 %copy-done.4 = bf16[2,1,2,256,256]{4,3,2,1,0:T(8,128)(2,1)S(1)} copy-done((bf16[2,1,2,256,256]{4,3,2,1,0:T(8,128)(2,1)S(1)}, bf16[2,1,2,256,256]{4,3,2,1,0:T(8,128)(2,1)}, u32[]{:S(2)}) %copy-start.4) | copy-done | bytes 524312
  72.6 3.9 %shard_map.56.refs_10_ = bf16[2,1,2,256,2560]{4,3,2,1,0:T(8,128)(2,1)} custom-call(s32[16]{0:T(128)S(1)} %reshape.192.refs_0_, s32[2]{0:T(128)S(1)} %iota_add_fusion.refs_1_, bf16[2,4,1,2,256,256]{5,4,3,2,1,0:T(8,128)(2,1)S(1)} %copy-done, bf16[2,1,2,256,256]{4,3,2,1,0:T(8,128)(2,1)S(1)} %copy-done.4, ...), custom_call_target="tpu_custom_call", output_to_operand_aliasing={{}: (7, {})} | custom-call | flops 1073741824 | bytes 5242880 | tf_op jit(solution)/shard_map/pallas_call | solution.py:99
  76.6 5.0 %shard_map.57 = bf16[2,1,2,256,2560]{4,3,2,1,0:T(8,128)(2,1)} custom-call(s32[32]{0:T(128)S(1)} %pad_add_fusion.refs_0_, s32[4]{0:T(128)S(1)} %pad_add_fusion.1.refs_1_, bf16[2,4,1,2,256,256]{5,4,3,2,1,0:T(8,128)(2,1)S(1)} %copy-done, bf16[2,1,2,256,256]{4,3,2,1,0:T(8,128)(2,1)S(1)} %copy-done.2, ...), custom_call_target="tpu_custom_call", output_to_operand_aliasing={{}: (10, {})} | custom-call | flops 2147483648 | bytes 8388608 | tf_op jit(solution)/shard_map/pallas_call | solution.py:99
  (52 shorter events, 1.6 us)
Async XLA Ops:
  0.0 5.7 %copy-start.5 = (s32[2,4]{1,0:T(2,128)S(1)}, s32[2,4]{1,0:T(2,128)}, u32[]{:S(2)}) copy-start(s32[2,4]{1,0:T(2,128)} %param.8) | copy-start | bytes 100
  0.0 5.7 %copy-start.7 = (s32[2]{0:T(128)S(1)}, s32[2]{0:T(128)}, u32[]{:S(2)}) copy-start(s32[2]{0:T(128)} %param.9) | copy-start | bytes 28
  1.1 13.8 %collective-permute-start.3 = (bf16[2,1,2,256,256]{4,3,2,1,0:T(8,128)(2,1)S(1)}, bf16[2,1,2,256,256]{4,3,2,1,0:T(8,128)(2,1)S(1)}, u32[]{:S(2)}, u32[]{:S(2)}) collective-permute-start(bf16[2,1,2,256,256]{4,3,2,1,0:T(8,128)(2,1)S(1)} %slice.52), channel_id=1, source_target_pairs={{0,2},{1,3},{2,0},{3,1},{4,6},{5,7},{6,4},{7,5},{8,10},{9,11},{10,... | collective-permute-start | bytes 1572872 | tf_op jit(solution)/shard_map/ppermute | solution.py:149
  5.9 20.9 %collective-permute-start = (bf16[2,1,2,272,256]{4,3,2,1,0:T(8,128)(2,1)S(1)}, bf16[2,1,2,272,256]{4,3,2,1,0:T(8,128)(2,1)S(1)}, u32[]{:S(2)}, u32[]{:S(2)}) collective-permute-start(bf16[2,1,2,272,256]{4,3,2,1,0:T(8,128)(2,1)S(1)} %pad_maximum_fusion.1), channel_id=1, source_target_pairs={{0,2},{1,3},{2,0},{3,1},{4,6},{5,7},{6,4},{7,5},{8,10},{9,11},{10,... | collective-permute-start | bytes 1671176 | tf_op jit(solution)/shard_map/ppermute | solution.py:149
  14.9 37.7 %copy-start.3 = (bf16[2,1,2,256,256]{4,3,2,1,0:T(8,128)(2,1)}, bf16[2,1,2,256,256]{4,3,2,1,0:T(8,128)(2,1)S(1)}, u32[]{:S(2)}) copy-start(bf16[2,1,2,256,256]{4,3,2,1,0:T(8,128)(2,1)S(1)} %collective-permute-done.3.refs_3_) | copy-start | bytes 1572868
  14.9 23.3 %collective-permute-start.5 = (bf16[2,1,2,256,256]{4,3,2,1,0:T(8,128)(2,1)}, bf16[2,1,2,256,256]{4,3,2,1,0:T(8,128)(2,1)}, u32[]{:S(2)}, u32[]{:S(2)}) collective-permute-start(bf16[2,1,2,256,256]{4,3,2,1,0:T(8,128)(2,1)} %get-tuple-element.21), channel_id=1, source_target_pairs={{0,2},{1,3},{2,0},{3,1},{4,6},{5,7},{6,4},{7,5},{8,10},{9,11},{10,... | collective-permute-start | bytes 1572872 | tf_op jit(solution)/shard_map/ppermute | solution.py:149
  16.0 24.2 %collective-permute-start.4 = (bf16[2,1,2,256,256]{4,3,2,1,0:T(8,128)(2,1)S(1)}, bf16[2,1,2,256,256]{4,3,2,1,0:T(8,128)(2,1)S(1)}, u32[]{:S(2)}, u32[]{:S(2)}) collective-permute-start(bf16[2,1,2,256,256]{4,3,2,1,0:T(8,128)(2,1)S(1)} %collective-permute-done.3.refs_3_), channel_id=1, source_target_pairs={{0,4},{1,5},{2,14},{3,15},{4,8},{5,9},{6,2},{7,3},{8,12},{9,13},{1... | collective-permute-start | bytes 1572872 | tf_op jit(solution)/shard_map/ppermute | solution.py:149
  26.8 33.1 %collective-permute-start.10 = (bf16[8,1,2,256,256]{4,3,2,1,0:T(8,128)(2,1)}, bf16[8,1,2,256,256]{4,3,2,1,0:T(8,128)(2,1)}, u32[]{:S(2)}, u32[]{:S(2)}) collective-permute-start(bf16[8,1,2,256,256]{4,3,2,1,0:T(8,128)(2,1)} %bitcast.refs_3_), channel_id=1, source_target_pairs={{0,1},{1,0},{2,3},{3,2},{4,5},{5,4},{6,7},{7,6},{8,9},{9,8},{10,11... | collective-permute-start | bytes 6291464 | tf_op jit(solution)/shard_map/ppermute | solution.py:149
  29.0 21.6 %collective-permute-start.1 = (bf16[2,1,2,272,256]{4,3,2,1,0:T(8,128)(2,1)S(1)}, bf16[2,1,2,272,256]{4,3,2,1,0:T(8,128)(2,1)S(1)}, u32[]{:S(2)}, u32[]{:S(2)}) collective-permute-start(bf16[2,1,2,272,256]{4,3,2,1,0:T(8,128)(2,1)S(1)} %collective-permute-done.refs_4_), channel_id=1, source_target_pairs={{0,4},{1,5},{2,14},{3,15},{4,8},{5,9},{6,2},{7,3},{8,12},{9,13},{1... | collective-permute-start | bytes 1671176 | tf_op jit(solution)/shard_map/ppermute | solution.py:149
  30.8 18.6 %collective-permute-start.7 = (bf16[2,1,2,256,256]{4,3,2,1,0:T(8,128)(2,1)}, bf16[2,1,2,256,256]{4,3,2,1,0:T(8,128)(2,1)}, u32[]{:S(2)}, u32[]{:S(2)}) collective-permute-start(bf16[2,1,2,256,256]{4,3,2,1,0:T(8,128)(2,1)} %get-tuple-element.22), channel_id=1, source_target_pairs={{0,2},{1,3},{2,0},{3,1},{4,6},{5,7},{6,4},{7,5},{8,10},{9,11},{10,... | collective-permute-start | bytes 1572872 | tf_op jit(solution)/shard_map/ppermute | solution.py:149
  38.2 16.7 %collective-permute-start.9 = (s32[2,4]{1,0:T(2,128)S(1)}, s32[2,4]{1,0:T(2,128)S(1)}, u32[]{:S(2)}, u32[]{:S(2)}) collective-permute-start(s32[2,4]{1,0:T(2,128)S(1)} %get-tuple-element.23), channel_id=1, source_target_pairs={{0,1},{1,0},{2,3},{3,2},{4,5},{5,4},{6,7},{7,6},{8,9},{9,8},{10,11... | collective-permute-start | bytes 104 | tf_op jit(solution)/shard_map/ppermute | solution.py:149
  40.2 12.3 %copy-start.1 = (bf16[2,1,2,256,256]{4,3,2,1,0:T(8,128)(2,1)}, bf16[2,1,2,256,256]{4,3,2,1,0:T(8,128)(2,1)S(1)}, u32[]{:S(2)}) copy-start(bf16[2,1,2,256,256]{4,3,2,1,0:T(8,128)(2,1)S(1)} %collective-permute-done.4.refs_3_) | copy-start | bytes 1572868
  40.2 16.9 %collective-permute-start.6 = (bf16[2,1,2,256,256]{4,3,2,1,0:T(8,128)(2,1)}, bf16[2,1,2,256,256]{4,3,2,1,0:T(8,128)(2,1)}, u32[]{:S(2)}, u32[]{:S(2)}) collective-permute-start(bf16[2,1,2,256,256]{4,3,2,1,0:T(8,128)(2,1)} %collective-permute-done.5.refs_5_), channel_id=1, source_target_pairs={{0,4},{1,5},{2,14},{3,15},{4,8},{5,9},{6,2},{7,3},{8,12},{9,13},{1... | collective-permute-start | bytes 1572872 | tf_op jit(solution)/shard_map/ppermute | solution.py:149
  42.9 12.0 %copy-start.6 = (s32[2,4]{1,0:T(2,128)S(1)}, s32[2,4]{1,0:T(2,128)}, u32[]{:S(2)}) copy-start(s32[2,4]{1,0:T(2,128)} %param.6) | copy-start | bytes 100
  49.4 19.0 %collective-permute-start.8 = (bf16[2,1,2,256,256]{4,3,2,1,0:T(8,128)(2,1)}, bf16[2,1,2,256,256]{4,3,2,1,0:T(8,128)(2,1)}, u32[]{:S(2)}, u32[]{:S(2)}) collective-permute-start(bf16[2,1,2,256,256]{4,3,2,1,0:T(8,128)(2,1)} %collective-permute-done.7.refs_6_), channel_id=1, source_target_pairs={{0,4},{1,5},{2,14},{3,15},{4,8},{5,9},{6,2},{7,3},{8,12},{9,13},{1... | collective-permute-start | bytes 1572872 | tf_op jit(solution)/shard_map/ppermute | solution.py:149
  50.7 4.2 %collective-permute-start.2 = (s32[2,4]{1,0:T(2,128)S(1)}, s32[2,4]{1,0:T(2,128)S(1)}, u32[]{:S(2)}, u32[]{:S(2)}) collective-permute-start(s32[2,4]{1,0:T(2,128)S(1)} %broadcast_select_fusion.3), channel_id=1, source_target_pairs={{0,1},{1,0},{2,3},{3,2},{4,5},{5,4},{6,7},{7,6},{8,9},{9,8},{10,11... | collective-permute-start | bytes 104 | tf_op jit(solution)/shard_map/ppermute | solution.py:149
  52.6 7.3 %copy-start = (bf16[2,4,1,2,256,256]{5,4,3,2,1,0:T(8,128)(2,1)S(1)}, bf16[2,4,1,2,256,256]{5,4,3,2,1,0:T(8,128)(2,1)}, u32[]{:S(2)}) copy-start(bf16[2,4,1,2,256,256]{5,4,3,2,1,0:T(8,128)(2,1)} %refs_2_.5) | copy-start | bytes 6291460
  54.9 21.6 %collective-permute-start.11 = (bf16[4,1,2,256,256]{4,3,2,1,0:T(8,128)(2,1)}, bf16[4,1,2,256,256]{4,3,2,1,0:T(8,128)(2,1)}, u32[]{:S(2)}, u32[]{:S(2)}) collective-permute-start(bf16[4,1,2,256,256]{4,3,2,1,0:T(8,128)(2,1)} %pad_maximum_fusion), channel_id=1, source_target_pairs={{0,1},{1,0},{2,3},{3,2},{4,5},{5,4},{6,7},{7,6},{8,9},{9,8},{10,11... | collective-permute-start | bytes 3145736 | tf_op jit(solution)/shard_map/ppermute | solution.py:149
  59.1 17.5 %collective-permute-start.12 = (bf16[2,1,2,256,256]{4,3,2,1,0:T(8,128)(2,1)}, bf16[2,1,2,256,256]{4,3,2,1,0:T(8,128)(2,1)}, u32[]{:S(2)}, u32[]{:S(2)}) collective-permute-start(bf16[2,1,2,256,256]{4,3,2,1,0:T(8,128)(2,1)} %broadcast_select_fusion.1), channel_id=1, source_target_pairs={{0,1},{1,0},{2,3},{3,2},{4,5},{5,4},{6,7},{7,6},{8,9},{9,8},{10,11... | collective-permute-start | bytes 1572872 | tf_op jit(solution)/shard_map/ppermute | solution.py:149
  70.3 6.3 %collective-permute-start.13 = (bf16[2,1,2,256,256]{4,3,2,1,0:T(8,128)(2,1)}, bf16[2,1,2,256,256]{4,3,2,1,0:T(8,128)(2,1)}, u32[]{:S(2)}, u32[]{:S(2)}) collective-permute-start(bf16[2,1,2,256,256]{4,3,2,1,0:T(8,128)(2,1)} %broadcast_select_fusion), channel_id=1, source_target_pairs={{0,1},{1,0},{2,3},{3,2},{4,5},{5,4},{6,7},{7,6},{8,9},{9,8},{10,11... | collective-permute-start | bytes 1572872 | tf_op jit(solution)/shard_map/ppermute | solution.py:149
  71.6 1.1 %copy-start.4 = (bf16[2,1,2,256,256]{4,3,2,1,0:T(8,128)(2,1)S(1)}, bf16[2,1,2,256,256]{4,3,2,1,0:T(8,128)(2,1)}, u32[]{:S(2)}) copy-start(bf16[2,1,2,256,256]{4,3,2,1,0:T(8,128)(2,1)} %copy-done.3) | copy-start | bytes 1572868
  72.6 3.9 %copy-start.2 = (bf16[2,1,2,256,256]{4,3,2,1,0:T(8,128)(2,1)S(1)}, bf16[2,1,2,256,256]{4,3,2,1,0:T(8,128)(2,1)}, u32[]{:S(2)}) copy-start(bf16[2,1,2,256,256]{4,3,2,1,0:T(8,128)(2,1)} %copy-done.1) | copy-start | bytes 1572868

commit v3 on v0

v3 whole, which is shorter than its diff:
```python
import functools

import jax
import jax.numpy as jnp
from jax import lax
from jax.experimental import pallas as pl
from jax.experimental.pallas import tpu as pltpu
from jax.sharding import PartitionSpec as P

HALF = 2
CHUNK = 2
ONWARD = 3
EARLY = (3, 2)
VMEM_BYTES = 56 * 2**20


def gather_kernel(count, table_ref, own_ref, other_ref, *refs):
    *out_refs, held, sem, out_sem = refs
    chunk = out_refs[0].shape[0]

    def inward(source_ref, t):
        return pltpu.make_async_copy(source_ref.at[table_ref[2 * t + 1]], held.at[t], sem.at[t])

    def outward(t):
        target = out_refs[t // chunk].at[t % chunk]
        return pltpu.make_async_copy(held.at[t], target, out_sem.at[t])

    for t in range(count):

        @pl.when(table_ref[2 * t] == 0)
        def _():
            inward(own_ref, t).start()

        @pl.when(table_ref[2 * t] != 0)
        def _():
            inward(other_ref, t).start()

    for t in range(count):
        inward(own_ref, t).wait()
        outward(t).start()
    for t in range(count):
        outward(t).wait()


def gathered(table, own, other, chunks):
    shape = jax.ShapeDtypeStruct((CHUNK,) + own.shape[1:], own.dtype)
    any_spec = pl.BlockSpec(memory_space=pltpu.HBM)
    return pl.pallas_call(
        functools.partial(gather_kernel, chunks * CHUNK),
        out_shape=[shape] * chunks,
        in_specs=[pl.BlockSpec(memory_space=pltpu.SMEM), any_spec, any_spec],
        out_specs=[any_spec] * chunks,
        scratch_shapes=[
            pltpu.VMEM((chunks * CHUNK,) + own.shape[1:], own.dtype),
            pltpu.SemaphoreType.DMA((chunks * CHUNK,)),
            pltpu.SemaphoreType.DMA((chunks * CHUNK,)),
        ],
        compiler_params=pltpu.CompilerParams(vmem_limit_bytes=VMEM_BYTES),
    )(table, own, other)


def product_kernel(groups, slots, positions, total_positions, aliased, *refs):
    table_ref, slab_v = refs[:2]
    chunk_refs = refs[2 : 2 + len(positions)]
    refs = refs[2 + len(positions) + aliased :]
    out_ref, block_v, total, out_v, block_sem, out_sem = refs
    rows, _, freqs = slab_v.shape[:3]
    side = slab_v.shape[4]

    def match(b, r):
        return table_ref[total_positions + b * rows + r]

    def place(g):
        return table_ref[total_positions + groups * slots * rows + g]

    for start, ref in zip(positions, chunk_refs):
        for i in range(ref.shape[0]):
            target = table_ref[start + i]

            @pl.when(target >= 0)
            def _():
                pltpu.make_async_copy(
                    ref.at[i], block_v.at[target], block_sem.at[target]
                ).start()

    def out_copy(g, r):
        columns = pl.ds(pl.multiple_of(place(g) * side, side), side)
        return pltpu.make_async_copy(
            out_v.at[g, r], out_ref.at[r, :, :, :, columns], out_sem.at[g, r]
        )

    def product(b, r, own, p):
        for f in range(freqs):
            real, imag = block_v[b, f, 0], block_v[b, f, 1]
            both = jnp.concatenate([slab_v[r, own, f, 0], slab_v[r, own, f, 1]], axis=1)
            right = jnp.concatenate((imag, real) if p else (real, -imag))
            yield f, jnp.dot(both, right, preferred_element_type=jnp.float32)

    def row_panel(g, r):
        hits = [match(g * slots + j, r) for j in range(slots)]
        found = sum((hit >= 0).astype(jnp.int32) for hit in hits)

        @pl.when(found == 0)
        def _():
            out_v[g, r] = jnp.zeros(out_v.shape[2:], out_v.dtype)

        @pl.when(found == 1)
        def _():
            own = functools.reduce(jnp.maximum, hits)
            j = sum(jnp.where(hit >= 0, j, 0) for j, hit in enumerate(hits))
            for p in range(2):
                for f, value in product(g * slots + j, r, own, p):
                    out_v[g, r, f, p] = value.astype(out_v.dtype)

        @pl.when(found > 1)
        def _():
            total[...] = jnp.zeros_like(total)

            def add(j, carry):
                own = match(g * slots + j, r)

                @pl.when(own >= 0)
                def _():
                    for p in range(2):
                        for f, value in product(g * slots + j, r, own, p):
                            total[f, p] += value

                return carry

            lax.fori_loop(0, slots, add, 0)
            out_v[g, r] = total[...].astype(out_v.dtype)

        out_copy(g, r).start()

    def group(g, carry):
        @pl.when(place(g) >= 0)
        def _():
            for j in range(slots):
                b = g * slots + j

                @pl.when(functools.reduce(jnp.maximum, [match(b, r) for r in range(rows)]) >= 0)
                def _():
                    pltpu.make_async_copy(block_v.at[b], block_v.at[b], block_sem.at[b]).wait()

            for r in range(rows):
                row_panel(g, r)

        return carry

    def drain(g, carry):
        @pl.when(place(g) >= 0)
        def _():
            for r in range(rows):
                out_copy(g, r).wait()

        return carry

    lax.fori_loop(0, groups, group, 0)
    lax.fori_loop(0, groups, drain, 0)


def products(slab, table, groups, slots, total_positions, sources, out_shape, before=None):
    rows, _, freqs, parts, side, _ = slab.shape
    any_spec = pl.BlockSpec(memory_space=pltpu.HBM)
    operands = [table, slab, *(c for _, c in sources)] + ([] if before is None else [before])
    kernel = functools.partial(
        product_kernel, groups, slots, [p for p, _ in sources], total_positions, before is not None
    )
    return pl.pallas_call(
        kernel,
        out_shape=out_shape,
        in_specs=[pl.BlockSpec(memory_space=pltpu.SMEM), pl.BlockSpec(memory_space=pltpu.VMEM)]
        + [any_spec] * (len(operands) - 2),
        out_specs=any_spec,
        scratch_shapes=[
            pltpu.VMEM((groups * slots, freqs, parts, side, side), slab.dtype),
            pltpu.VMEM((freqs, parts, side, side), jnp.float32),
            pltpu.VMEM((groups, rows, freqs, parts, side, side), out_shape.dtype),
            pltpu.SemaphoreType.DMA((groups * slots,)),
            pltpu.SemaphoreType.DMA((groups, rows)),
        ],
        input_output_aliases={} if before is None else {len(operands) - 1: 0},
        compiler_params=pltpu.CompilerParams(vmem_limit_bytes=VMEM_BYTES),
    )(*operands)


def after(value, *others):
    return lax.optimization_barrier((value, *others))


def stations(rows, chip, cols, slots, devices):
    blocks = cols * slots
    index = jnp.arange(2 * blocks, dtype=jnp.int32)
    first = index % slots == 0
    reach = 2 * devices
    away = (rows - (4 * chip[..., None] + 2) + devices) % reach - devices
    away = jnp.where(chip[..., None] % 2 == 0, away, -away)
    key = jnp.where(rows >= 0, away, reach) * (2 * blocks) + index
    before = (key[..., None, :] < key[..., :, None]) & ~first
    rank = jnp.sum(before.astype(jnp.int32), axis=-1)
    own = index // blocks * blocks + index % blocks // slots
    dealt = rank % 2 * blocks + cols + rank // 2
    return jnp.where(first, own, dealt)


def shards(slab, slab_cols, panels, panel_rows, panel_live):
    rows, _, freqs, parts, side, _ = slab.shape
    cols, slots = panel_rows.shape
    count = cols * slots
    chunks = count // CHUNK
    devices = lax.axis_size("blk")
    chips = devices // 2
    me = lax.axis_index("blk")
    core, chip = me % 2, me // 2
    toward = jnp.where(chip % 2 == 0, 1, -1)

    def permuted(value, target):
        return lax.ppermute(value, "blk", [(i, target(i)) for i in range(devices)])

    def partner_chip(i):
        return i ^ 2

    def partner_core(i):
        return i ^ 1

    def onward(i):
        return (i + 4 if (i // 2) % 2 == 0 else i - 4) % devices

    live = jnp.arange(slots, dtype=jnp.int32)[None, :] < panel_live[:, None]
    own_rows = jnp.where(live, panel_rows, -1).reshape(-1)
    own_lists = jnp.concatenate([own_rows, slab_cols.reshape(-1)])[None]

    def doubled(lists):
        size = lists.shape[0]
        others = permuted(lists, lambda i: i ^ size)
        low = (me // size) % 2 == 0
        return jnp.where(
            low, jnp.concatenate([lists, others]), jnp.concatenate([others, lists])
        )

    blocks = panels.reshape((count,) + panels.shape[2:])
    across = [permuted(panels[:, 0], partner_chip)]
    lists = doubled(own_lists)
    other = permuted(blocks, partner_core)

    pair = lists[:, :count].reshape(-1)
    other_rows = jnp.where(core == 0, lists[1, :count], lists[0, :count])
    station = stations(pair, chip, cols, slots, devices)
    wanted = core * count + jnp.arange(CHUNK, count, dtype=jnp.int32)
    index = jnp.arange(2 * count, dtype=jnp.int32)
    picked = jnp.sum(jnp.where(station[None] == wanted[:, None], index, 0), axis=1)
    table = jnp.stack([jnp.abs(picked // count - core), picked % count], axis=1).reshape(-1)
    pieces = list(gathered(table, blocks, other, chunks - 1))

    across.append(permuted(pieces[0], partner_chip))
    for k in range(2, chunks):
        if k == 2:
            lists = doubled(lists)
            lists, pieces[k - 1] = after(lists, pieces[k - 1])
        across[k - 2], pieces[k - 1] = after(across[k - 2], pieces[k - 1])
        across.append(permuted(pieces[k - 1], partner_chip))
    along = [permuted(across[k], onward) for k in range(ONWARD - 1)]
    while lists.shape[0] < devices:
        lists = doubled(lists)
    across[ONWARD - 1], lists = after(across[ONWARD - 1], lists)
    along.append(permuted(across[ONWARD - 1], onward))

    all_rows = lists[:, :count].reshape(chips, 2 * count)
    all_cols = lists[:, count:].reshape(chips, 2, -1)
    all_chips = jnp.arange(chips, dtype=jnp.int32)
    all_stations = stations(all_rows, all_chips, cols, slots, devices)

    def meets(found):
        same = found[..., None, None] == slab_cols
        order = jnp.arange(slab_cols.shape[1], dtype=jnp.int32)
        return jnp.max(jnp.where(same, order, -1), axis=-1)

    out_shape = jax.ShapeDtypeStruct(
        (rows, freqs, parts, side, (2 * HALF + 1) * cols * side), jnp.bfloat16
    )
    q = jnp.arange(cols, dtype=jnp.int32)

    def table_of(position, match, place, total_positions):
        match = jnp.where((place >= 0)[:, None, None], match, -1)
        used = jnp.any(match >= 0, axis=-1).reshape(-1)
        at = jnp.arange(total_positions, dtype=jnp.int32)
        here = (position.reshape(-1)[None, :] == at[:, None]) & used
        target = jnp.max(jnp.where(here, jnp.arange(used.size, dtype=jnp.int32), -1), axis=1)
        return jnp.concatenate([target, match.reshape(-1), place]).astype(jnp.int32)

    near = jnp.stack([jnp.zeros_like(me), 1 - 2 * core])
    place = ((near + HALF)[:, None] * cols + q).reshape(-1)
    position = jnp.arange(2 * count, dtype=jnp.int32).reshape(2 * cols, slots)
    match = meets(jnp.concatenate([own_rows, other_rows]).reshape(2 * cols, slots))
    out = products(
        slab,
        table_of(position, match, place, 2 * count),
        2 * cols,
        slots,
        2 * count,
        [(0, blocks), (count, other)],
        out_shape,
    )

    sources = jnp.stack([chip + toward, (chip - toward) % chips])
    offset = jnp.stack([2 * toward, -2 * toward])[:, None] + jnp.arange(2) - core
    found = all_rows[sources].reshape(4 * cols, slots)
    station = all_stations[sources]
    position = station % count + jnp.where(station // count == core, 0, count)
    position += 2 * count * jnp.arange(2, dtype=jnp.int32)[:, None]
    position = position.reshape(4 * cols, slots)
    match = meets(found)
    match = jnp.where((found >= 0)[..., None], match, -1)
    place = jnp.where(jnp.abs(offset) <= HALF, offset + HALF, -1)
    place = jnp.where(place[..., None] >= 0, place[..., None] * cols + q, -1).reshape(-1)
    used = jnp.any(match >= 0, axis=-1)
    turn = position % count // CHUNK
    from_z = position >= 2 * count

    def ready(limits):
        return jnp.all(~used | (turn < jnp.where(from_z, limits[1], limits[0])), axis=1)

    early, usual = ready(EARLY), ready((chunks, ONWARD))
    total_positions = 4 * count

    def step(chosen, parts_held, before):
        sources = [
            (kind * count + k * CHUNK, c) for kind, held in enumerate(parts_held) for k, c in enumerate(held)
        ]
        table = table_of(position, match, jnp.where(chosen, place, -1), total_positions)
        return products(
            slab, table, 4 * cols, slots, total_positions, sources, out_shape, before
        )

    across_other = [permuted(c, partner_core) for c in across]
    along_other = [permuted(c, partner_core) for c in along]
    a, b = EARLY
    held = (across, across_other, along, along_other)
    out = step(usual, held, out)

    late = all_stations % count // CHUNK >= ONWARD
    back = jnp.where(all_chips % 2 == 0, -1, 1)
    readers = all_cols[(all_chips + back) % chips]
    hit = jnp.any(all_rows[:, :, None, None] == readers[:, None], axis=-1)
    of_core = index[:, None] // count - jnp.arange(2)
    within = jnp.abs(of_core - 2 * back[:, None, None]) <= HALF
    rare = jnp.any(hit & within & (late & (all_rows >= 0))[..., None])

    def complete(out):
        more = [permuted(c, onward) for c in across[ONWARD:]]
        more_other = [permuted(c, partner_core) for c in more]
        return step(~usual, (across, across_other, along + more, along_other + more_other), out)

    return lax.cond(rare, complete, lambda out: out, out)


def solution(mesh):
    placed = (
        P(("grp", "blk"), None, None, None, None, None),
        P("blk", None),
        P(("grp", "blk"), None, None, None, None, None),
        P("blk", None),
        P("blk"),
    )
    return jax.shard_map(
        shards,
        mesh=mesh,
        in_specs=placed,
        out_specs=P(("grp", "blk"), None, None, None, None),
        check_vma=False,
    )
```

time: 217 us -> 76.1 us (0.35); the launches traced: 213 us -> 75.8 us
  other arithmetic: 77.3 us -> 6.58 us
  matrix products: 37.1 us -> 0 us
  waiting for transfers between devices: 48.4 us -> 24.1 us
  local copies, waits for them, and re-layouts: 29.3 us -> 6.42 us
  Pallas kernels: 0 us -> 13.9 us
  starting transfers between devices: 20.7 us -> 24 us
    another operation x15 -> x2, other arithmetic: 69.9 us -> 0.08 us  [the longest x1 0.07 us: shards(): jnp.stack([2 * toward, -2 * toward])[:, None] + jnp.arange(2) - core]
    dot_general x10 -> x0, matrix products: 37.1 us -> none  [the longest x5 24.6 us: block_products(): jnp.einsum('rcjopfax,cjfpxb->rfoacb', stacked, panel_blocks, preferred_el...]
    ppermute x12 -> x19, waiting for transfers between devices: 48.4 us -> 24.1 us  [permuted(): return lax.ppermute(value, 'blk', [(i, target(i)) for i in range(devices)])]
    unnamed x30 -> x4, local copies, waits for them, and re-layouts: 20 us -> 0.01 us
    pallas_call x0 -> x3, Pallas kernels: none -> 13.9 us  [the longest x2 11 us: products(): pl.pallas_call(kernel, out_shape=out_shape, in_specs=[pl.BlockSpec(memory...]
    concatenate x2 -> x0, local copies, waits for them, and re-layouts: 9.01 us -> none  [shards(): return jnp.concatenate(ordered, axis=4)]
    neg x5 -> x0, other arithmetic: 7.05 us -> none  [block_products(): -imag_part]
    ppermute x12 -> x19, starting transfers between devices: 20.7 us -> 24 us  [permuted(): return lax.ppermute(value, 'blk', [(i, target(i)) for i in range(devices)])]
  transfers between devices with their start and end apart: 12 -> 19, of which waited for: 4 -> 6; matrix products, arithmetic and copies ran while one was open for 60% -> 15% of each run, Pallas kernels for 0% -> 9%
where the time goes in v3:
time: 76.1 us; the launch traced here: 75.8 us
  waiting for transfers between devices  24.1 us (32%)
  starting transfers between devices  24 us (32%)
  Pallas kernels  13.9 us (18%)
  other arithmetic  6.58 us (9%)
  local copies, waits for them, and re-layouts  6.42 us (8%)
  between operations  0.84 us (1%)
    ppermute x19, waiting for transfers between devices, permuted(): return lax.ppermute(value, 'blk', [(i, target(i)) for i in range(devices)])  24.1 us
    ppermute x19, starting transfers between devices, permuted(): return lax.ppermute(value, 'blk', [(i, target(i)) for i in range(devices)])  24 us
    pallas_call x2, Pallas kernels, products(): pl.pallas_call(kernel, out_shape=out_shape, in_specs=[pl.BlockSpec(memory...  11 us
    pallas_call x1, Pallas kernels, gathered(): pl.pallas_call(functools.partial(gather_kernel, chunks * CHUNK), out_shap...  2.85 us
  transfers between devices with their start and end apart: 19, of which 6 were waited for; matrix products, arithmetic and copies ran while one was open for 15% of the time, Pallas kernels for 9%

profile of v3, /device:TPU:1, one launch (start us, length us, event | category | flops | bytes accessed | tf_op | source)
XLA Modules:
  0.0 75.8 jit_solution(18433475384612447160)
XLA Ops:
  0.0 0.9 %reshape.927 = s32[8]{0:T(128)S(1)} reshape(s32[2,4]{1,0:T(2,128)} %param.8) | data formatting | bytes 64 | tf_op jit(solution)/shard_map/reshape | solution.py:231
  0.9 0.8 compare_select_fusion.10
  1.9 1.1 %slice_bitcast_fusion = bf16[2,1,2,256,256]{4,3,2,1,0:T(8,128)(2,1)S(1)} fusion(bf16[2,4,1,2,256,256]{5,4,3,2,1,0:T(8,128)(2,1)} %param.9), kind=kLoop, calls=%fused_computation.19 | loop fusion | bytes 1048576 | tf_op jit(solution)/shard_map/squeeze | solution.py:242
  3.0 2.8 %collective-permute-start.2 = (bf16[2,1,2,256,256]{4,3,2,1,0:T(8,128)(2,1)S(1)}, bf16[2,1,2,256,256]{4,3,2,1,0:T(8,128)(2,1)S(1)}, u32[]{:S(2)}, u32[]{:S(2)}) collective-permute-start(bf16[2,1,2,256,256]{4,3,2,1,0:T(8,128)(2,1)S(1)} %slice_bitcast_fusion), channel_id=1, source_target_pairs={{0,2},{1,3},{2,0},{3,1},{4,6},{5,7},{6,4},{7,5},{8,10},{9,11},{10,... | collective-permute-start | bytes 1572872 | tf_op jit(solution)/shard_map/ppermute | solution.py:218
  6.3 0.8 fusion.55
  8.7 1.0 %select_reduce_fusion.1 = s32[4,4,2]{1,2,0:T(2,128)S(1)} fusion(s32[2,4]{1,0:T(2,128)} %param.8, s32[4,4]{1,0:T(4,128)S(1)} %add_bitcast_fusion), kind=kLoop, calls=%fused_computation.22 | loop fusion | flops 352 | bytes 224 | tf_op jit(solution)/shard_map/reduce_max | solution.py:276
  9.8 0.6 reshape.928.table_ref
  10.4 7.6 %collective-permute-done.4 = s32[2,16]{1,0:T(2,128)S(1)} collective-permute-done((s32[2,16]{1,0:T(2,128)S(1)}, s32[2,16]{1,0:T(2,128)S(1)}, u32[]{:S(2)}, u32[]{:S(2)}) %collective-permute-start.4) | collective-permute-done | bytes 160 | tf_op jit(solution)/shard_map/ppermute | solution.py:218
  18.0 2.8 %shard_map.57 = (bf16[2,1,2,256,256]{4,3,2,1,0:T(8,128)(2,1)}, bf16[2,1,2,256,256]{4,3,2,1,0:T(8,128)(2,1)}, bf16[2,1,2,256,256]{4,3,2,1,0:T(8,128)(2,1)}) custom-call(s32[12]{0:T(128)} %reshape.928.table_ref, bf16[8,1,2,256,256]{4,3,2,1,0:T(8,128)(2,1)} %bitcast.42, bf16[8,1,2,256,256]{4,3,2,1,0:T(8,128)(2,1)} %collective-permute-done.5.other_ref.refs_3_), custom_call_target="tpu_custom_call" | custom-call | tf_op jit(solution)/shard_map/pallas_call | solution.py:48
  20.9 1.3 %collective-permute-start.6 = (bf16[2,1,2,256,256]{4,3,2,1,0:T(8,128)(2,1)}, bf16[2,1,2,256,256]{4,3,2,1,0:T(8,128)(2,1)S(1)}, u32[]{:S(2)}, u32[]{:S(2)}) collective-permute-start(bf16[2,1,2,256,256]{4,3,2,1,0:T(8,128)(2,1)} %get-tuple-element.148), channel_id=1, source_target_pairs={{0,2},{1,3},{2,0},{3,1},{4,6},{5,7},{6,4},{7,5},{8,10},{9,11},{10,... | collective-permute-start | bytes 1572872 | tf_op jit(solution)/shard_map/ppermute | solution.py:218
  22.4 1.3 %collective-permute-start.7 = (s32[4,16]{1,0:T(4,128)S(1)}, s32[4,16]{1,0:T(4,128)S(1)}, u32[]{:S(2)}, u32[]{:S(2)}) collective-permute-start(s32[4,16]{1,0:T(4,128)S(1)} %add_select_fusion.11), channel_id=1, source_target_pairs={{0,4},{1,5},{2,6},{3,7},{4,0},{5,1},{6,2},{7,3},{8,12},{9,13},{10,... | collective-permute-start | bytes 776 | tf_op jit(solution)/shard_map/ppermute | solution.py:218
  24.0 1.1 %collective-permute-done.7 = s32[4,16]{1,0:T(4,128)S(1)} collective-permute-done((s32[4,16]{1,0:T(4,128)S(1)}, s32[4,16]{1,0:T(4,128)S(1)}, u32[]{:S(2)}, u32[]{:S(2)}) %collective-permute-start.7) | collective-permute-done | bytes 288 | tf_op jit(solution)/shard_map/ppermute | solution.py:218
  25.2 2.1 %collective-permute-start.8 = (s32[8,16]{1,0:T(8,128)S(1)}, s32[8,16]{1,0:T(8,128)S(1)}, u32[]{:S(2)}, u32[]{:S(2)}) collective-permute-start(s32[8,16]{1,0:T(8,128)S(1)} %add_select_fusion.6), channel_id=1, source_target_pairs={{0,8},{1,9},{2,10},{3,11},{4,12},{5,13},{6,14},{7,15},{8,0},{9,1},... | collective-permute-start | bytes 1544 | tf_op jit(solution)/shard_map/ppermute | solution.py:218
  27.8 1.3 %collective-permute-start.15 = (bf16[2,1,2,256,256]{4,3,2,1,0:T(8,128)(2,1)S(1)}, bf16[2,1,2,256,256]{4,3,2,1,0:T(8,128)(2,1)}, u32[]{:S(2)}, u32[]{:S(2)}) collective-permute-start(bf16[2,1,2,256,256]{4,3,2,1,0:T(8,128)(2,1)S(1)} %collective-permute-done.2.refs_2_), channel_id=1, source_target_pairs={{0,4},{1,5},{2,14},{3,15},{4,8},{5,9},{6,2},{7,3},{8,12},{9,13},{1... | collective-permute-start | bytes 1572872 | tf_op jit(solution)/shard_map/ppermute | solution.py:218
  29.1 2.8 %collective-permute-start.11 = (bf16[2,1,2,256,256]{4,3,2,1,0:T(8,128)(2,1)S(1)}, bf16[2,1,2,256,256]{4,3,2,1,0:T(8,128)(2,1)}, u32[]{:S(2)}, u32[]{:S(2)}) collective-permute-start(bf16[2,1,2,256,256]{4,3,2,1,0:T(8,128)(2,1)S(1)} %collective-permute-done.2.refs_2_), channel_id=1, source_target_pairs={{0,1},{1,0},{2,3},{3,2},{4,5},{5,4},{6,7},{7,6},{8,9},{9,8},{10,11... | collective-permute-start | bytes 1572872 | tf_op jit(solution)/shard_map/ppermute | solution.py:218
  31.9 4.2 %shard_map.58.refs_16_ = bf16[2,1,2,256,2560]{4,3,2,1,0:T(8,128)(2,1)} custom-call(s32[52]{0:T(128)} %pad_add_fusion.4.refs_0_, bf16[2,4,1,2,256,256]{5,4,3,2,1,0:T(8,128)(2,1)S(1)} %copy-done, bf16[8,1,2,256,256]{4,3,2,1,0:T(8,128)(2,1)} %bitcast.43, bf16[8,1,2,256,256]{4,3,2,1,0:T(8,128)(2,1)} %collective-permute-done.5.other_ref.refs_3_), custom_call_target="tpu_custom_call" | custom-call | tf_op jit(solution)/shard_map/pallas_call | solution.py:169
  36.4 0.6 gather_fusion.2
  38.0 2.0 %collective-permute-start.17 = (bf16[2,1,2,256,256]{4,3,2,1,0:T(8,128)(2,1)S(1)}, bf16[2,1,2,256,256]{4,3,2,1,0:T(8,128)(2,1)}, u32[]{:S(2)}, u32[]{:S(2)}) collective-permute-start(bf16[2,1,2,256,256]{4,3,2,1,0:T(8,128)(2,1)S(1)} %collective-permute-done.6.refs_4_), channel_id=1, source_target_pairs={{0,4},{1,5},{2,14},{3,15},{4,8},{5,9},{6,2},{7,3},{8,12},{9,13},{1... | collective-permute-start | bytes 1572872 | tf_op jit(solution)/shard_map/ppermute | solution.py:218
  40.0 1.1 %collective-permute-start.13 = (bf16[2,1,2,256,256]{4,3,2,1,0:T(8,128)(2,1)S(1)}, bf16[2,1,2,256,256]{4,3,2,1,0:T(8,128)(2,1)}, u32[]{:S(2)}, u32[]{:S(2)}) collective-permute-start(bf16[2,1,2,256,256]{4,3,2,1,0:T(8,128)(2,1)S(1)} %collective-permute-done.6.refs_4_), channel_id=1, source_target_pairs={{0,1},{1,0},{2,3},{3,2},{4,5},{5,4},{6,7},{7,6},{8,9},{9,8},{10,11... | collective-permute-start | bytes 1572872 | tf_op jit(solution)/shard_map/ppermute | solution.py:218
  41.4 0.6 gather_fusion
  42.0 4.2 %collective-permute-done.9.refs_3_ = bf16[2,1,2,256,256]{4,3,2,1,0:T(8,128)(2,1)} collective-permute-done((bf16[2,1,2,256,256]{4,3,2,1,0:T(8,128)(2,1)}, bf16[2,1,2,256,256]{4,3,2,1,0:T(8,128)(2,1)}, u32[]{:S(2)}, u32[]{:S(2)}) %collective-permute-start.9) | collective-permute-done | bytes 524320 | tf_op jit(solution)/shard_map/ppermute | solution.py:218
  46.5 1.3 %collective-permute-start.16 = (bf16[2,1,2,256,256]{4,3,2,1,0:T(8,128)(2,1)}, bf16[2,1,2,256,256]{4,3,2,1,0:T(8,128)(2,1)}, u32[]{:S(2)}, u32[]{:S(2)}) collective-permute-start(bf16[2,1,2,256,256]{4,3,2,1,0:T(8,128)(2,1)} %collective-permute-done.9.refs_3_), channel_id=1, source_target_pairs={{0,4},{1,5},{2,14},{3,15},{4,8},{5,9},{6,2},{7,3},{8,12},{9,13},{1... | collective-permute-start | bytes 1572872 | tf_op jit(solution)/shard_map/ppermute | solution.py:218
  48.0 2.4 %collective-permute-start.12 = (bf16[2,1,2,256,256]{4,3,2,1,0:T(8,128)(2,1)}, bf16[2,1,2,256,256]{4,3,2,1,0:T(8,128)(2,1)}, u32[]{:S(2)}, u32[]{:S(2)}) collective-permute-start(bf16[2,1,2,256,256]{4,3,2,1,0:T(8,128)(2,1)} %collective-permute-done.9.refs_3_), channel_id=1, source_target_pairs={{0,1},{1,0},{2,3},{3,2},{4,5},{5,4},{6,7},{7,6},{8,9},{9,8},{10,11... | collective-permute-start | bytes 1572872 | tf_op jit(solution)/shard_map/ppermute | solution.py:218
  50.3 3.6 %collective-permute-done.17.refs_12_ = bf16[2,1,2,256,256]{4,3,2,1,0:T(8,128)(2,1)} collective-permute-done((bf16[2,1,2,256,256]{4,3,2,1,0:T(8,128)(2,1)S(1)}, bf16[2,1,2,256,256]{4,3,2,1,0:T(8,128)(2,1)}, u32[]{:S(2)}, u32[]{:S(2)}) %collective-permute-start.17) | collective-permute-done | bytes 524320 | tf_op jit(solution)/shard_map/ppermute | solution.py:218
  54.0 2.2 %collective-permute-start.18 = (bf16[2,1,2,256,256]{4,3,2,1,0:T(8,128)(2,1)}, bf16[2,1,2,256,256]{4,3,2,1,0:T(8,128)(2,1)}, u32[]{:S(2)}, u32[]{:S(2)}) collective-permute-start(bf16[2,1,2,256,256]{4,3,2,1,0:T(8,128)(2,1)} %collective-permute-done.15.refs_10_), channel_id=1, source_target_pairs={{0,1},{1,0},{2,3},{3,2},{4,5},{5,4},{6,7},{7,6},{8,9},{9,8},{10,11... | collective-permute-start | bytes 1572872 | tf_op jit(solution)/shard_map/ppermute | solution.py:218
  56.2 3.2 %collective-permute-done.10.refs_5_ = bf16[2,1,2,256,256]{4,3,2,1,0:T(8,128)(2,1)} collective-permute-done((bf16[2,1,2,256,256]{4,3,2,1,0:T(8,128)(2,1)}, bf16[2,1,2,256,256]{4,3,2,1,0:T(8,128)(2,1)}, u32[]{:S(2)}, u32[]{:S(2)}) %collective-permute-start.10) | collective-permute-done | bytes 524320 | tf_op jit(solution)/shard_map/ppermute | solution.py:218
  59.4 1.5 %collective-permute-start.14 = (bf16[2,1,2,256,256]{4,3,2,1,0:T(8,128)(2,1)}, bf16[2,1,2,256,256]{4,3,2,1,0:T(8,128)(2,1)}, u32[]{:S(2)}, u32[]{:S(2)}) collective-permute-start(bf16[2,1,2,256,256]{4,3,2,1,0:T(8,128)(2,1)} %collective-permute-done.10.refs_5_), channel_id=1, source_target_pairs={{0,1},{1,0},{2,3},{3,2},{4,5},{5,4},{6,7},{7,6},{8,9},{9,8},{10,11... | collective-permute-start | bytes 1572872 | tf_op jit(solution)/shard_map/ppermute | solution.py:218
  60.9 4.3 %collective-permute-done.16.refs_11_ = bf16[2,1,2,256,256]{4,3,2,1,0:T(8,128)(2,1)} collective-permute-done((bf16[2,1,2,256,256]{4,3,2,1,0:T(8,128)(2,1)}, bf16[2,1,2,256,256]{4,3,2,1,0:T(8,128)(2,1)}, u32[]{:S(2)}, u32[]{:S(2)}) %collective-permute-start.16) | collective-permute-done | bytes 524320 | tf_op jit(solution)/shard_map/ppermute | solution.py:218
  65.2 1.3 %collective-permute-start.19 = (bf16[2,1,2,256,256]{4,3,2,1,0:T(8,128)(2,1)}, bf16[2,1,2,256,256]{4,3,2,1,0:T(8,128)(2,1)}, u32[]{:S(2)}, u32[]{:S(2)}) collective-permute-start(bf16[2,1,2,256,256]{4,3,2,1,0:T(8,128)(2,1)} %collective-permute-done.16.refs_11_), channel_id=1, source_target_pairs={{0,1},{1,0},{2,3},{3,2},{4,5},{5,4},{6,7},{7,6},{8,9},{9,8},{10,11... | collective-permute-start | bytes 1572872 | tf_op jit(solution)/shard_map/ppermute | solution.py:218
  66.5 0.7 fusion.7
  68.4 0.6 pad_add_fusion.3.refs_0_
  69.0 6.8 %shard_map.59 = bf16[2,1,2,256,2560]{4,3,2,1,0:T(8,128)(2,1)} custom-call(s32[104]{0:T(128)} %pad_add_fusion.3.refs_0_, bf16[2,4,1,2,256,256]{5,4,3,2,1,0:T(8,128)(2,1)S(1)} %copy-done, bf16[2,1,2,256,256]{4,3,2,1,0:T(8,128)(2,1)S(1)} %collective-permute-done.2.refs_2_, ...), custom_call_target="tpu_custom_call", output_to_operand_aliasing={{}: (16, {})} | custom-call | tf_op jit(solution)/shard_map/pallas_call | solution.py:169
  (101 shorter events, 6.2 us)
Async XLA Ops:
  0.0 31.9 %copy-start = (bf16[2,4,1,2,256,256]{5,4,3,2,1,0:T(8,128)(2,1)S(1)}, bf16[2,4,1,2,256,256]{5,4,3,2,1,0:T(8,128)(2,1)}, u32[]{:S(2)}) copy-start(bf16[2,4,1,2,256,256]{5,4,3,2,1,0:T(8,128)(2,1)} %refs_1_.3) | copy-start | bytes 6291460
  1.8 6.1 %collective-permute-start.3 = (s32[1,16]{1,0:T(1,128)S(1)}, s32[1,16]{1,0:T(1,128)S(1)}, u32[]{:S(2)}, u32[]{:S(2)}) collective-permute-start(s32[1,16]{1,0:T(1,128)S(1)} %add_bitcast_fusion.1), channel_id=1, source_target_pairs={{0,1},{1,0},{2,3},{3,2},{4,5},{5,4},{6,7},{7,6},{8,9},{9,8},{10,11... | collective-permute-start | bytes 200 | tf_op jit(solution)/shard_map/ppermute | solution.py:218
  3.0 17.9 %collective-permute-start.2 = (bf16[2,1,2,256,256]{4,3,2,1,0:T(8,128)(2,1)S(1)}, bf16[2,1,2,256,256]{4,3,2,1,0:T(8,128)(2,1)S(1)}, u32[]{:S(2)}, u32[]{:S(2)}) collective-permute-start(bf16[2,1,2,256,256]{4,3,2,1,0:T(8,128)(2,1)S(1)} %slice_bitcast_fusion), channel_id=1, source_target_pairs={{0,2},{1,3},{2,0},{3,1},{4,6},{5,7},{6,4},{7,5},{8,10},{9,11},{10,... | collective-permute-start | bytes 1572872 | tf_op jit(solution)/shard_map/ppermute | solution.py:218
  5.7 12.3 %collective-permute-start.5 = (bf16[8,1,2,256,256]{4,3,2,1,0:T(8,128)(2,1)}, bf16[8,1,2,256,256]{4,3,2,1,0:T(8,128)(2,1)}, u32[]{:S(2)}, u32[]{:S(2)}) collective-permute-start(bf16[8,1,2,256,256]{4,3,2,1,0:T(8,128)(2,1)} %bitcast.41), channel_id=1, source_target_pairs={{0,1},{1,0},{2,3},{3,2},{4,5},{5,4},{6,7},{7,6},{8,9},{9,8},{10,11... | collective-permute-start | bytes 6291464 | tf_op jit(solution)/shard_map/ppermute | solution.py:218
  7.9 10.1 %collective-permute-start.4 = (s32[2,16]{1,0:T(2,128)S(1)}, s32[2,16]{1,0:T(2,128)S(1)}, u32[]{:S(2)}, u32[]{:S(2)}) collective-permute-start(s32[2,16]{1,0:T(2,128)S(1)} %add_select_fusion.13), channel_id=1, source_target_pairs={{0,2},{1,3},{2,0},{3,1},{4,6},{5,7},{6,4},{7,5},{8,10},{9,11},{10,... | collective-permute-start | bytes 392 | tf_op jit(solution)/shard_map/ppermute | solution.py:218
  20.9 15.3 %collective-permute-start.6 = (bf16[2,1,2,256,256]{4,3,2,1,0:T(8,128)(2,1)}, bf16[2,1,2,256,256]{4,3,2,1,0:T(8,128)(2,1)S(1)}, u32[]{:S(2)}, u32[]{:S(2)}) collective-permute-start(bf16[2,1,2,256,256]{4,3,2,1,0:T(8,128)(2,1)} %get-tuple-element.148), channel_id=1, source_target_pairs={{0,2},{1,3},{2,0},{3,1},{4,6},{5,7},{6,4},{7,5},{8,10},{9,11},{10,... | collective-permute-start | bytes 1572872 | tf_op jit(solution)/shard_map/ppermute | solution.py:218
  22.4 2.7 %collective-permute-start.7 = (s32[4,16]{1,0:T(4,128)S(1)}, s32[4,16]{1,0:T(4,128)S(1)}, u32[]{:S(2)}, u32[]{:S(2)}) collective-permute-start(s32[4,16]{1,0:T(4,128)S(1)} %add_select_fusion.11), channel_id=1, source_target_pairs={{0,4},{1,5},{2,6},{3,7},{4,0},{5,1},{6,2},{7,3},{8,12},{9,13},{10,... | collective-permute-start | bytes 776 | tf_op jit(solution)/shard_map/ppermute | solution.py:218
  25.2 11.0 %collective-permute-start.8 = (s32[8,16]{1,0:T(8,128)S(1)}, s32[8,16]{1,0:T(8,128)S(1)}, u32[]{:S(2)}, u32[]{:S(2)}) collective-permute-start(s32[8,16]{1,0:T(8,128)S(1)} %add_select_fusion.6), channel_id=1, source_target_pairs={{0,8},{1,9},{2,10},{3,11},{4,12},{5,13},{6,14},{7,15},{8,0},{9,1},... | collective-permute-start | bytes 1544 | tf_op jit(solution)/shard_map/ppermute | solution.py:218
  27.8 18.7 %collective-permute-start.15 = (bf16[2,1,2,256,256]{4,3,2,1,0:T(8,128)(2,1)S(1)}, bf16[2,1,2,256,256]{4,3,2,1,0:T(8,128)(2,1)}, u32[]{:S(2)}, u32[]{:S(2)}) collective-permute-start(bf16[2,1,2,256,256]{4,3,2,1,0:T(8,128)(2,1)S(1)} %collective-permute-done.2.refs_2_), channel_id=1, source_target_pairs={{0,4},{1,5},{2,14},{3,15},{4,8},{5,9},{6,2},{7,3},{8,12},{9,13},{1... | collective-permute-start | bytes 1572872 | tf_op jit(solution)/shard_map/ppermute | solution.py:218
  29.1 18.9 %collective-permute-start.11 = (bf16[2,1,2,256,256]{4,3,2,1,0:T(8,128)(2,1)S(1)}, bf16[2,1,2,256,256]{4,3,2,1,0:T(8,128)(2,1)}, u32[]{:S(2)}, u32[]{:S(2)}) collective-permute-start(bf16[2,1,2,256,256]{4,3,2,1,0:T(8,128)(2,1)S(1)} %collective-permute-done.2.refs_2_), channel_id=1, source_target_pairs={{0,1},{1,0},{2,3},{3,2},{4,5},{5,4},{6,7},{7,6},{8,9},{9,8},{10,11... | collective-permute-start | bytes 1572872 | tf_op jit(solution)/shard_map/ppermute | solution.py:218
  31.9 14.5 %copy-start.1 = (s32[2,4]{1,0:T(2,128)S(1)}, s32[2,4]{1,0:T(2,128)}, u32[]{:S(2)}) copy-start(s32[2,4]{1,0:T(2,128)} %param.8) | copy-start | bytes 100
  31.9 14.3 %collective-permute-start.9 = (bf16[2,1,2,256,256]{4,3,2,1,0:T(8,128)(2,1)}, bf16[2,1,2,256,256]{4,3,2,1,0:T(8,128)(2,1)}, u32[]{:S(2)}, u32[]{:S(2)}) collective-permute-start(bf16[2,1,2,256,256]{4,3,2,1,0:T(8,128)(2,1)} %get-tuple-element.152), channel_id=1, source_target_pairs={{0,2},{1,3},{2,0},{3,1},{4,6},{5,7},{6,4},{7,5},{8,10},{9,11},{10,... | collective-permute-start | bytes 1572872 | tf_op jit(solution)/shard_map/ppermute | solution.py:218
  38.0 15.9 %collective-permute-start.17 = (bf16[2,1,2,256,256]{4,3,2,1,0:T(8,128)(2,1)S(1)}, bf16[2,1,2,256,256]{4,3,2,1,0:T(8,128)(2,1)}, u32[]{:S(2)}, u32[]{:S(2)}) collective-permute-start(bf16[2,1,2,256,256]{4,3,2,1,0:T(8,128)(2,1)S(1)} %collective-permute-done.6.refs_4_), channel_id=1, source_target_pairs={{0,4},{1,5},{2,14},{3,15},{4,8},{5,9},{6,2},{7,3},{8,12},{9,13},{1... | collective-permute-start | bytes 1572872 | tf_op jit(solution)/shard_map/ppermute | solution.py:218
  40.0 16.2 %collective-permute-start.13 = (bf16[2,1,2,256,256]{4,3,2,1,0:T(8,128)(2,1)S(1)}, bf16[2,1,2,256,256]{4,3,2,1,0:T(8,128)(2,1)}, u32[]{:S(2)}, u32[]{:S(2)}) collective-permute-start(bf16[2,1,2,256,256]{4,3,2,1,0:T(8,128)(2,1)S(1)} %collective-permute-done.6.refs_4_), channel_id=1, source_target_pairs={{0,1},{1,0},{2,3},{3,2},{4,5},{5,4},{6,7},{7,6},{8,9},{9,8},{10,11... | collective-permute-start | bytes 1572872 | tf_op jit(solution)/shard_map/ppermute | solution.py:218
  46.2 13.2 %collective-permute-start.10 = (bf16[2,1,2,256,256]{4,3,2,1,0:T(8,128)(2,1)}, bf16[2,1,2,256,256]{4,3,2,1,0:T(8,128)(2,1)}, u32[]{:S(2)}, u32[]{:S(2)}) collective-permute-start(bf16[2,1,2,256,256]{4,3,2,1,0:T(8,128)(2,1)} %get-tuple-element.156), channel_id=1, source_target_pairs={{0,2},{1,3},{2,0},{3,1},{4,6},{5,7},{6,4},{7,5},{8,10},{9,11},{10,... | collective-permute-start | bytes 1572872 | tf_op jit(solution)/shard_map/ppermute | solution.py:218
  46.5 18.7 %collective-permute-start.16 = (bf16[2,1,2,256,256]{4,3,2,1,0:T(8,128)(2,1)}, bf16[2,1,2,256,256]{4,3,2,1,0:T(8,128)(2,1)}, u32[]{:S(2)}, u32[]{:S(2)}) collective-permute-start(bf16[2,1,2,256,256]{4,3,2,1,0:T(8,128)(2,1)} %collective-permute-done.9.refs_3_), channel_id=1, source_target_pairs={{0,4},{1,5},{2,14},{3,15},{4,8},{5,9},{6,2},{7,3},{8,12},{9,13},{1... | collective-permute-start | bytes 1572872 | tf_op jit(solution)/shard_map/ppermute | solution.py:218
  48.0 21.0 %collective-permute-start.12 = (bf16[2,1,2,256,256]{4,3,2,1,0:T(8,128)(2,1)}, bf16[2,1,2,256,256]{4,3,2,1,0:T(8,128)(2,1)}, u32[]{:S(2)}, u32[]{:S(2)}) collective-permute-start(bf16[2,1,2,256,256]{4,3,2,1,0:T(8,128)(2,1)} %collective-permute-done.9.refs_3_), channel_id=1, source_target_pairs={{0,1},{1,0},{2,3},{3,2},{4,5},{5,4},{6,7},{7,6},{8,9},{9,8},{10,11... | collective-permute-start | bytes 1572872 | tf_op jit(solution)/shard_map/ppermute | solution.py:218
  54.0 15.0 %collective-permute-start.18 = (bf16[2,1,2,256,256]{4,3,2,1,0:T(8,128)(2,1)}, bf16[2,1,2,256,256]{4,3,2,1,0:T(8,128)(2,1)}, u32[]{:S(2)}, u32[]{:S(2)}) collective-permute-start(bf16[2,1,2,256,256]{4,3,2,1,0:T(8,128)(2,1)} %collective-permute-done.15.refs_10_), channel_id=1, source_target_pairs={{0,1},{1,0},{2,3},{3,2},{4,5},{5,4},{6,7},{7,6},{8,9},{9,8},{10,11... | collective-permute-start | bytes 1572872 | tf_op jit(solution)/shard_map/ppermute | solution.py:218
  56.2 12.8 %collective-permute-start.20 = (bf16[2,1,2,256,256]{4,3,2,1,0:T(8,128)(2,1)}, bf16[2,1,2,256,256]{4,3,2,1,0:T(8,128)(2,1)}, u32[]{:S(2)}, u32[]{:S(2)}) collective-permute-start(bf16[2,1,2,256,256]{4,3,2,1,0:T(8,128)(2,1)} %collective-permute-done.17.refs_12_), channel_id=1, source_target_pairs={{0,1},{1,0},{2,3},{3,2},{4,5},{5,4},{6,7},{7,6},{8,9},{9,8},{10,11... | collective-permute-start | bytes 1572872 | tf_op jit(solution)/shard_map/ppermute | solution.py:218
  59.4 9.6 %collective-permute-start.14 = (bf16[2,1,2,256,256]{4,3,2,1,0:T(8,128)(2,1)}, bf16[2,1,2,256,256]{4,3,2,1,0:T(8,128)(2,1)}, u32[]{:S(2)}, u32[]{:S(2)}) collective-permute-start(bf16[2,1,2,256,256]{4,3,2,1,0:T(8,128)(2,1)} %collective-permute-done.10.refs_5_), channel_id=1, source_target_pairs={{0,1},{1,0},{2,3},{3,2},{4,5},{5,4},{6,7},{7,6},{8,9},{9,8},{10,11... | collective-permute-start | bytes 1572872 | tf_op jit(solution)/shard_map/ppermute | solution.py:218
  65.2 3.8 %collective-permute-start.19 = (bf16[2,1,2,256,256]{4,3,2,1,0:T(8,128)(2,1)}, bf16[2,1,2,256,256]{4,3,2,1,0:T(8,128)(2,1)}, u32[]{:S(2)}, u32[]{:S(2)}) collective-permute-start(bf16[2,1,2,256,256]{4,3,2,1,0:T(8,128)(2,1)} %collective-permute-done.16.refs_11_), channel_id=1, source_target_pairs={{0,1},{1,0},{2,3},{3,2},{4,5},{5,4},{6,7},{7,6},{8,9},{9,8},{10,11... | collective-permute-start | bytes 1572872 | tf_op jit(solution)/shard_map/ppermute | solution.py:218

commit v4 on v3

--- a/solution.py
+++ b/solution.py
@@ -239,7 +239,8 @@
         )
 
     blocks = panels.reshape((count,) + panels.shape[2:])
-    across = [permuted(panels[:, 0], partner_chip)]
+    piece, own_lists = after(panels[:, 0], own_lists)
+    across = [permuted(piece, partner_chip)]
     lists = doubled(own_lists)
     other = permuted(blocks, partner_core)
 
@@ -254,7 +255,7 @@
 
     across.append(permuted(pieces[0], partner_chip))
     for k in range(2, chunks):
-        if k == 2:
+        if k == 3:
             lists = doubled(lists)
             lists, pieces[k - 1] = after(lists, pieces[k - 1])
         across[k - 2], pieces[k - 1] = after(across[k - 2], pieces[k - 1])

time: 76.1 us -> 72.1 us (0.947)
  starting transfers between devices: 24 us -> 20.8 us
  waiting for transfers between devices: 24.1 us -> 23.3 us
    ppermute x19, starting transfers between devices: 24 us -> 20.8 us  [permuted(): return lax.ppermute(value, 'blk', [(i, target(i)) for i in range(devices)])]
  transfers between devices with their start and end apart: 19 -> 19, of which waited for: 6 -> 6; matrix products, arithmetic and copies ran while one was open for 15% -> 14% of each run, Pallas kernels for 9% -> 11%
where the time goes in v4:
time: 72.1 us; the launch traced here: 72.4 us
  waiting for transfers between devices  23.3 us (32%)
  starting transfers between devices  20.8 us (29%)
  Pallas kernels  14.5 us (20%)
  other arithmetic  6.57 us (9%)
  local copies, waits for them, and re-layouts  6.42 us (9%)
  between operations  0.82 us (1%)
    ppermute x19, waiting for transfers between devices, permuted(): return lax.ppermute(value, 'blk', [(i, target(i)) for i in range(devices)])  23.3 us
    ppermute x19, starting transfers between devices, permuted(): return lax.ppermute(value, 'blk', [(i, target(i)) for i in range(devices)])  20.8 us
    pallas_call x2, Pallas kernels, products(): pl.pallas_call(kernel, out_shape=out_shape, in_specs=[pl.BlockSpec(memory...  11.6 us
    pallas_call x1, Pallas kernels, gathered(): pl.pallas_call(functools.partial(gather_kernel, chunks * CHUNK), out_shap...  2.84 us
  transfers between devices with their start and end apart: 19, of which 6 were waited for; matrix products, arithmetic and copies ran while one was open for 14% of the time, Pallas kernels for 11%

profile of v4, /device:TPU:1, one launch (start us, length us, event | category | flops | bytes accessed | tf_op | source)
XLA Modules:
  0.0 72.4 jit_solution(18205140378321029975)
XLA Ops:
  0.0 0.9 %reshape.927 = s32[8]{0:T(128)S(1)} reshape(s32[2,4]{1,0:T(2,128)} %param.8) | data formatting | bytes 64 | tf_op jit(solution)/shard_map/reshape | solution.py:231
  0.9 0.8 %compare_select_fusion.10 = s32[2,4]{1,0:T(2,128)S(1)} fusion(s32[2,4]{1,0:T(2,128)} %param.10, s32[2]{0:T(128)} %param.11), kind=kLoop, calls=%fused_computation.133 | loop fusion | flops 16 | bytes 72 | tf_op jit(solution)/shard_map/jit(_where)/select_n | solution.py:230
  1.7 1.1 %slice_bitcast_fusion = bf16[2,1,2,256,256]{4,3,2,1,0:T(8,128)(2,1)S(1)} fusion(bf16[2,4,1,2,256,256]{5,4,3,2,1,0:T(8,128)(2,1)} %param.9), kind=kLoop, calls=%fused_computation.19 | loop fusion | bytes 1048576 | tf_op jit(solution)/shard_map/squeeze | solution.py:242
  3.0 2.7 %collective-permute-start.2 = (bf16[2,1,2,256,256]{4,3,2,1,0:T(8,128)(2,1)S(1)}, bf16[2,1,2,256,256]{4,3,2,1,0:T(8,128)(2,1)S(1)}, u32[]{:S(2)}, u32[]{:S(2)}) collective-permute-start(bf16[2,1,2,256,256]{4,3,2,1,0:T(8,128)(2,1)S(1)} %slice_bitcast_fusion), channel_id=1, source_target_pairs={{0,2},{1,3},{2,0},{3,1},{4,6},{5,7},{6,4},{7,5},{8,10},{9,11},{10,... | collective-permute-start | bytes 1572872 | tf_op jit(solution)/shard_map/ppermute | solution.py:218
  6.3 0.8 %fusion.55 = s32[2,4,1,1]{1,0,3,2:T(2,128)S(1)} fusion(s32[2,4]{1,0:T(2,128)} %param.10, s32[2]{0:T(128)} %param.11), kind=kLoop, calls=%fused_computation.196 | loop fusion | flops 16 | bytes 72 | tf_op jit(solution)/shard_map/concatenate | solution.py:295
  8.5 1.0 %select_reduce_fusion.1 = s32[4,4,2]{1,2,0:T(2,128)S(1)} fusion(s32[2,4]{1,0:T(2,128)} %param.8, s32[4,4]{1,0:T(4,128)S(1)} %add_bitcast_fusion), kind=kLoop, calls=%fused_computation.22 | loop fusion | flops 352 | bytes 224 | tf_op jit(solution)/shard_map/reduce_max | solution.py:277
  10.0 0.6 reshape.928.table_ref
  10.6 2.8 %shard_map.57 = (bf16[2,1,2,256,256]{4,3,2,1,0:T(8,128)(2,1)}, bf16[2,1,2,256,256]{4,3,2,1,0:T(8,128)(2,1)}, bf16[2,1,2,256,256]{4,3,2,1,0:T(8,128)(2,1)}) custom-call(s32[12]{0:T(128)} %reshape.928.table_ref, bf16[8,1,2,256,256]{4,3,2,1,0:T(8,128)(2,1)} %bitcast.42, bf16[8,1,2,256,256]{4,3,2,1,0:T(8,128)(2,1)} %collective-permute-done.4.other_ref.refs_3_), custom_call_target="tpu_custom_call" | custom-call | tf_op jit(solution)/shard_map/pallas_call | solution.py:48
  13.4 4.4 %collective-permute-done.2.refs_2_ = bf16[2,1,2,256,256]{4,3,2,1,0:T(8,128)(2,1)S(1)} collective-permute-done((bf16[2,1,2,256,256]{4,3,2,1,0:T(8,128)(2,1)S(1)}, bf16[2,1,2,256,256]{4,3,2,1,0:T(8,128)(2,1)S(1)}, u32[]{:S(2)}, u32[]{:S(2)}) %collective-permute-start.2) | collective-permute-done | bytes 524320 | tf_op jit(solution)/shard_map/ppermute | solution.py:218
  17.9 1.3 %collective-permute-start.5 = (bf16[2,1,2,256,256]{4,3,2,1,0:T(8,128)(2,1)}, bf16[2,1,2,256,256]{4,3,2,1,0:T(8,128)(2,1)S(1)}, u32[]{:S(2)}, u32[]{:S(2)}) collective-permute-start(bf16[2,1,2,256,256]{4,3,2,1,0:T(8,128)(2,1)} %get-tuple-element.151), channel_id=1, source_target_pairs={{0,2},{1,3},{2,0},{3,1},{4,6},{5,7},{6,4},{7,5},{8,10},{9,11},{10,... | collective-permute-start | bytes 1572872 | tf_op jit(solution)/shard_map/ppermute | solution.py:218
  19.2 1.4 %collective-permute-start.7 = (s32[4,16]{1,0:T(4,128)S(1)}, s32[4,16]{1,0:T(4,128)S(1)}, u32[]{:S(2)}, u32[]{:S(2)}) collective-permute-start(s32[4,16]{1,0:T(4,128)S(1)} %add_select_fusion.11), channel_id=1, source_target_pairs={{0,4},{1,5},{2,6},{3,7},{4,0},{5,1},{6,2},{7,3},{8,12},{9,13},{10,... | collective-permute-start | bytes 776 | tf_op jit(solution)/shard_map/ppermute | solution.py:218
  20.9 1.1 %collective-permute-done.7 = s32[4,16]{1,0:T(4,128)S(1)} collective-permute-done((s32[4,16]{1,0:T(4,128)S(1)}, s32[4,16]{1,0:T(4,128)S(1)}, u32[]{:S(2)}, u32[]{:S(2)}) %collective-permute-start.7) | collective-permute-done | bytes 288 | tf_op jit(solution)/shard_map/ppermute | solution.py:218
  22.0 2.1 %collective-permute-start.8 = (s32[8,16]{1,0:T(8,128)S(1)}, s32[8,16]{1,0:T(8,128)S(1)}, u32[]{:S(2)}, u32[]{:S(2)}) collective-permute-start(s32[8,16]{1,0:T(8,128)S(1)} %add_select_fusion.6), channel_id=1, source_target_pairs={{0,8},{1,9},{2,10},{3,11},{4,12},{5,13},{6,14},{7,15},{8,0},{9,1},... | collective-permute-start | bytes 1544 | tf_op jit(solution)/shard_map/ppermute | solution.py:218
  24.6 1.3 %collective-permute-start.15 = (bf16[2,1,2,256,256]{4,3,2,1,0:T(8,128)(2,1)S(1)}, bf16[2,1,2,256,256]{4,3,2,1,0:T(8,128)(2,1)}, u32[]{:S(2)}, u32[]{:S(2)}) collective-permute-start(bf16[2,1,2,256,256]{4,3,2,1,0:T(8,128)(2,1)S(1)} %collective-permute-done.2.refs_2_), channel_id=1, source_target_pairs={{0,4},{1,5},{2,14},{3,15},{4,8},{5,9},{6,2},{7,3},{8,12},{9,13},{1... | collective-permute-start | bytes 1572872 | tf_op jit(solution)/shard_map/ppermute | solution.py:218
  25.9 2.9 %collective-permute-start.11 = (bf16[2,1,2,256,256]{4,3,2,1,0:T(8,128)(2,1)S(1)}, bf16[2,1,2,256,256]{4,3,2,1,0:T(8,128)(2,1)}, u32[]{:S(2)}, u32[]{:S(2)}) collective-permute-start(bf16[2,1,2,256,256]{4,3,2,1,0:T(8,128)(2,1)S(1)} %collective-permute-done.2.refs_2_), channel_id=1, source_target_pairs={{0,1},{1,0},{2,3},{3,2},{4,5},{5,4},{6,7},{7,6},{8,9},{9,8},{10,11... | collective-permute-start | bytes 1572872 | tf_op jit(solution)/shard_map/ppermute | solution.py:218
  28.8 5.1 %shard_map.58.refs_16_ = bf16[2,1,2,256,2560]{4,3,2,1,0:T(8,128)(2,1)} custom-call(s32[52]{0:T(128)} %pad_add_fusion.4.refs_0_, bf16[2,4,1,2,256,256]{5,4,3,2,1,0:T(8,128)(2,1)S(1)} %copy-done, bf16[8,1,2,256,256]{4,3,2,1,0:T(8,128)(2,1)} %bitcast.43, bf16[8,1,2,256,256]{4,3,2,1,0:T(8,128)(2,1)} %collective-permute-done.4.other_ref.refs_3_), custom_call_target="tpu_custom_call" | custom-call | tf_op jit(solution)/shard_map/pallas_call | solution.py:169
  34.1 0.6 gather_fusion.2
  35.0 0.6 gather_fusion.1
  35.7 0.6 collective-permute-start.17
  36.4 1.5 %collective-permute-start.13 = (bf16[2,1,2,256,256]{4,3,2,1,0:T(8,128)(2,1)S(1)}, bf16[2,1,2,256,256]{4,3,2,1,0:T(8,128)(2,1)}, u32[]{:S(2)}, u32[]{:S(2)}) collective-permute-start(bf16[2,1,2,256,256]{4,3,2,1,0:T(8,128)(2,1)S(1)} %collective-permute-done.5.refs_4_), channel_id=1, source_target_pairs={{0,1},{1,0},{2,3},{3,2},{4,5},{5,4},{6,7},{7,6},{8,9},{9,8},{10,11... | collective-permute-start | bytes 1572872 | tf_op jit(solution)/shard_map/ppermute | solution.py:218
  38.1 0.6 gather_fusion
  38.8 4.3 %collective-permute-done.9.refs_3_ = bf16[2,1,2,256,256]{4,3,2,1,0:T(8,128)(2,1)} collective-permute-done((bf16[2,1,2,256,256]{4,3,2,1,0:T(8,128)(2,1)}, bf16[2,1,2,256,256]{4,3,2,1,0:T(8,128)(2,1)}, u32[]{:S(2)}, u32[]{:S(2)}) %collective-permute-start.9) | collective-permute-done | bytes 524320 | tf_op jit(solution)/shard_map/ppermute | solution.py:218
  43.4 1.3 %collective-permute-start.16 = (bf16[2,1,2,256,256]{4,3,2,1,0:T(8,128)(2,1)}, bf16[2,1,2,256,256]{4,3,2,1,0:T(8,128)(2,1)}, u32[]{:S(2)}, u32[]{:S(2)}) collective-permute-start(bf16[2,1,2,256,256]{4,3,2,1,0:T(8,128)(2,1)} %collective-permute-done.9.refs_3_), channel_id=1, source_target_pairs={{0,4},{1,5},{2,14},{3,15},{4,8},{5,9},{6,2},{7,3},{8,12},{9,13},{1... | collective-permute-start | bytes 1572872 | tf_op jit(solution)/shard_map/ppermute | solution.py:218
  44.9 2.4 %collective-permute-start.12 = (bf16[2,1,2,256,256]{4,3,2,1,0:T(8,128)(2,1)}, bf16[2,1,2,256,256]{4,3,2,1,0:T(8,128)(2,1)}, u32[]{:S(2)}, u32[]{:S(2)}) collective-permute-start(bf16[2,1,2,256,256]{4,3,2,1,0:T(8,128)(2,1)} %collective-permute-done.9.refs_3_), channel_id=1, source_target_pairs={{0,1},{1,0},{2,3},{3,2},{4,5},{5,4},{6,7},{7,6},{8,9},{9,8},{10,11... | collective-permute-start | bytes 1572872 | tf_op jit(solution)/shard_map/ppermute | solution.py:218
  47.3 4.4 %collective-permute-done.17.refs_12_ = bf16[2,1,2,256,256]{4,3,2,1,0:T(8,128)(2,1)} collective-permute-done((bf16[2,1,2,256,256]{4,3,2,1,0:T(8,128)(2,1)S(1)}, bf16[2,1,2,256,256]{4,3,2,1,0:T(8,128)(2,1)}, u32[]{:S(2)}, u32[]{:S(2)}) %collective-permute-start.17) | collective-permute-done | bytes 524320 | tf_op jit(solution)/shard_map/ppermute | solution.py:218
  51.6 0.6 collective-permute-start.18
  52.2 4.0 %collective-permute-done.10.refs_5_ = bf16[2,1,2,256,256]{4,3,2,1,0:T(8,128)(2,1)} collective-permute-done((bf16[2,1,2,256,256]{4,3,2,1,0:T(8,128)(2,1)}, bf16[2,1,2,256,256]{4,3,2,1,0:T(8,128)(2,1)}, u32[]{:S(2)}, u32[]{:S(2)}) %collective-permute-start.10) | collective-permute-done | bytes 524320 | tf_op jit(solution)/shard_map/ppermute | solution.py:218
  56.2 1.5 %collective-permute-start.14 = (bf16[2,1,2,256,256]{4,3,2,1,0:T(8,128)(2,1)}, bf16[2,1,2,256,256]{4,3,2,1,0:T(8,128)(2,1)}, u32[]{:S(2)}, u32[]{:S(2)}) collective-permute-start(bf16[2,1,2,256,256]{4,3,2,1,0:T(8,128)(2,1)} %collective-permute-done.10.refs_5_), channel_id=1, source_target_pairs={{0,1},{1,0},{2,3},{3,2},{4,5},{5,4},{6,7},{7,6},{8,9},{9,8},{10,11... | collective-permute-start | bytes 1572872 | tf_op jit(solution)/shard_map/ppermute | solution.py:218
  57.7 5.1 %collective-permute-done.16.refs_11_ = bf16[2,1,2,256,256]{4,3,2,1,0:T(8,128)(2,1)} collective-permute-done((bf16[2,1,2,256,256]{4,3,2,1,0:T(8,128)(2,1)}, bf16[2,1,2,256,256]{4,3,2,1,0:T(8,128)(2,1)}, u32[]{:S(2)}, u32[]{:S(2)}) %collective-permute-start.16) | collective-permute-done | bytes 524320 | tf_op jit(solution)/shard_map/ppermute | solution.py:218
  63.4 0.7 fusion.7
  65.2 0.6 pad_add_fusion.3.refs_0_
  65.8 6.5 %shard_map.59 = bf16[2,1,2,256,2560]{4,3,2,1,0:T(8,128)(2,1)} custom-call(s32[104]{0:T(128)} %pad_add_fusion.3.refs_0_, bf16[2,4,1,2,256,256]{5,4,3,2,1,0:T(8,128)(2,1)S(1)} %copy-done, bf16[2,1,2,256,256]{4,3,2,1,0:T(8,128)(2,1)S(1)} %collective-permute-done.2.refs_2_, ...), custom_call_target="tpu_custom_call", output_to_operand_aliasing={{}: (16, {})} | custom-call | tf_op jit(solution)/shard_map/pallas_call | solution.py:169
  (101 shorter events, 6.2 us)
Async XLA Ops:
  0.0 28.8 %copy-start = (bf16[2,4,1,2,256,256]{5,4,3,2,1,0:T(8,128)(2,1)S(1)}, bf16[2,4,1,2,256,256]{5,4,3,2,1,0:T(8,128)(2,1)}, u32[]{:S(2)}) copy-start(bf16[2,4,1,2,256,256]{5,4,3,2,1,0:T(8,128)(2,1)} %refs_1_.3) | copy-start | bytes 6291460
  2.9 5.0 %collective-permute-start.3 = (s32[1,16]{1,0:T(1,128)S(1)}, s32[1,16]{1,0:T(1,128)S(1)}, u32[]{:S(2)}, u32[]{:S(2)}) collective-permute-start(s32[1,16]{1,0:T(1,128)S(1)} %add_bitcast_fusion.1), channel_id=1, source_target_pairs={{0,1},{1,0},{2,3},{3,2},{4,5},{5,4},{6,7},{7,6},{8,9},{9,8},{10,11... | collective-permute-start | bytes 200 | tf_op jit(solution)/shard_map/ppermute | solution.py:218
  3.0 14.9 %collective-permute-start.2 = (bf16[2,1,2,256,256]{4,3,2,1,0:T(8,128)(2,1)S(1)}, bf16[2,1,2,256,256]{4,3,2,1,0:T(8,128)(2,1)S(1)}, u32[]{:S(2)}, u32[]{:S(2)}) collective-permute-start(bf16[2,1,2,256,256]{4,3,2,1,0:T(8,128)(2,1)S(1)} %slice_bitcast_fusion), channel_id=1, source_target_pairs={{0,2},{1,3},{2,0},{3,1},{4,6},{5,7},{6,4},{7,5},{8,10},{9,11},{10,... | collective-permute-start | bytes 1572872 | tf_op jit(solution)/shard_map/ppermute | solution.py:218
  5.7 4.9 %collective-permute-start.4 = (bf16[8,1,2,256,256]{4,3,2,1,0:T(8,128)(2,1)}, bf16[8,1,2,256,256]{4,3,2,1,0:T(8,128)(2,1)}, u32[]{:S(2)}, u32[]{:S(2)}) collective-permute-start(bf16[8,1,2,256,256]{4,3,2,1,0:T(8,128)(2,1)} %bitcast.41), channel_id=1, source_target_pairs={{0,1},{1,0},{2,3},{3,2},{4,5},{5,4},{6,7},{7,6},{8,9},{9,8},{10,11... | collective-permute-start | bytes 6291464 | tf_op jit(solution)/shard_map/ppermute | solution.py:218
  7.9 11.2 %collective-permute-start.6 = (s32[2,16]{1,0:T(2,128)S(1)}, s32[2,16]{1,0:T(2,128)S(1)}, u32[]{:S(2)}, u32[]{:S(2)}) collective-permute-start(s32[2,16]{1,0:T(2,128)S(1)} %add_select_fusion.13), channel_id=1, source_target_pairs={{0,2},{1,3},{2,0},{3,1},{4,6},{5,7},{6,4},{7,5},{8,10},{9,11},{10,... | collective-permute-start | bytes 392 | tf_op jit(solution)/shard_map/ppermute | solution.py:218
  17.9 16.0 %collective-permute-start.5 = (bf16[2,1,2,256,256]{4,3,2,1,0:T(8,128)(2,1)}, bf16[2,1,2,256,256]{4,3,2,1,0:T(8,128)(2,1)S(1)}, u32[]{:S(2)}, u32[]{:S(2)}) collective-permute-start(bf16[2,1,2,256,256]{4,3,2,1,0:T(8,128)(2,1)} %get-tuple-element.151), channel_id=1, source_target_pairs={{0,2},{1,3},{2,0},{3,1},{4,6},{5,7},{6,4},{7,5},{8,10},{9,11},{10,... | collective-permute-start | bytes 1572872 | tf_op jit(solution)/shard_map/ppermute | solution.py:218
  19.2 2.8 %collective-permute-start.7 = (s32[4,16]{1,0:T(4,128)S(1)}, s32[4,16]{1,0:T(4,128)S(1)}, u32[]{:S(2)}, u32[]{:S(2)}) collective-permute-start(s32[4,16]{1,0:T(4,128)S(1)} %add_select_fusion.11), channel_id=1, source_target_pairs={{0,4},{1,5},{2,6},{3,7},{4,0},{5,1},{6,2},{7,3},{8,12},{9,13},{10,... | collective-permute-start | bytes 776 | tf_op jit(solution)/shard_map/ppermute | solution.py:218
  22.0 11.9 %collective-permute-start.8 = (s32[8,16]{1,0:T(8,128)S(1)}, s32[8,16]{1,0:T(8,128)S(1)}, u32[]{:S(2)}, u32[]{:S(2)}) collective-permute-start(s32[8,16]{1,0:T(8,128)S(1)} %add_select_fusion.6), channel_id=1, source_target_pairs={{0,8},{1,9},{2,10},{3,11},{4,12},{5,13},{6,14},{7,15},{8,0},{9,1},... | collective-permute-start | bytes 1544 | tf_op jit(solution)/shard_map/ppermute | solution.py:218
  24.6 18.8 %collective-permute-start.15 = (bf16[2,1,2,256,256]{4,3,2,1,0:T(8,128)(2,1)S(1)}, bf16[2,1,2,256,256]{4,3,2,1,0:T(8,128)(2,1)}, u32[]{:S(2)}, u32[]{:S(2)}) collective-permute-start(bf16[2,1,2,256,256]{4,3,2,1,0:T(8,128)(2,1)S(1)} %collective-permute-done.2.refs_2_), channel_id=1, source_target_pairs={{0,4},{1,5},{2,14},{3,15},{4,8},{5,9},{6,2},{7,3},{8,12},{9,13},{1... | collective-permute-start | bytes 1572872 | tf_op jit(solution)/shard_map/ppermute | solution.py:218
  25.9 19.0 %collective-permute-start.11 = (bf16[2,1,2,256,256]{4,3,2,1,0:T(8,128)(2,1)S(1)}, bf16[2,1,2,256,256]{4,3,2,1,0:T(8,128)(2,1)}, u32[]{:S(2)}, u32[]{:S(2)}) collective-permute-start(bf16[2,1,2,256,256]{4,3,2,1,0:T(8,128)(2,1)S(1)} %collective-permute-done.2.refs_2_), channel_id=1, source_target_pairs={{0,1},{1,0},{2,3},{3,2},{4,5},{5,4},{6,7},{7,6},{8,9},{9,8},{10,11... | collective-permute-start | bytes 1572872 | tf_op jit(solution)/shard_map/ppermute | solution.py:218
  28.8 14.5 %copy-start.1 = (s32[2,4]{1,0:T(2,128)S(1)}, s32[2,4]{1,0:T(2,128)}, u32[]{:S(2)}) copy-start(s32[2,4]{1,0:T(2,128)} %param.8) | copy-start | bytes 100
  28.8 14.3 %collective-permute-start.9 = (bf16[2,1,2,256,256]{4,3,2,1,0:T(8,128)(2,1)}, bf16[2,1,2,256,256]{4,3,2,1,0:T(8,128)(2,1)}, u32[]{:S(2)}, u32[]{:S(2)}) collective-permute-start(bf16[2,1,2,256,256]{4,3,2,1,0:T(8,128)(2,1)} %get-tuple-element.156), channel_id=1, source_target_pairs={{0,2},{1,3},{2,0},{3,1},{4,6},{5,7},{6,4},{7,5},{8,10},{9,11},{10,... | collective-permute-start | bytes 1572872 | tf_op jit(solution)/shard_map/ppermute | solution.py:218
  35.7 15.9 %collective-permute-start.17 = (bf16[2,1,2,256,256]{4,3,2,1,0:T(8,128)(2,1)S(1)}, bf16[2,1,2,256,256]{4,3,2,1,0:T(8,128)(2,1)}, u32[]{:S(2)}, u32[]{:S(2)}) collective-permute-start(bf16[2,1,2,256,256]{4,3,2,1,0:T(8,128)(2,1)S(1)} %collective-permute-done.5.refs_4_), channel_id=1, source_target_pairs={{0,4},{1,5},{2,14},{3,15},{4,8},{5,9},{6,2},{7,3},{8,12},{9,13},{1... | collective-permute-start | bytes 1572872 | tf_op jit(solution)/shard_map/ppermute | solution.py:218
  36.4 15.9 %collective-permute-start.13 = (bf16[2,1,2,256,256]{4,3,2,1,0:T(8,128)(2,1)S(1)}, bf16[2,1,2,256,256]{4,3,2,1,0:T(8,128)(2,1)}, u32[]{:S(2)}, u32[]{:S(2)}) collective-permute-start(bf16[2,1,2,256,256]{4,3,2,1,0:T(8,128)(2,1)S(1)} %collective-permute-done.5.refs_4_), channel_id=1, source_target_pairs={{0,1},{1,0},{2,3},{3,2},{4,5},{5,4},{6,7},{7,6},{8,9},{9,8},{10,11... | collective-permute-start | bytes 1572872 | tf_op jit(solution)/shard_map/ppermute | solution.py:218
  43.1 13.1 %collective-permute-start.10 = (bf16[2,1,2,256,256]{4,3,2,1,0:T(8,128)(2,1)}, bf16[2,1,2,256,256]{4,3,2,1,0:T(8,128)(2,1)}, u32[]{:S(2)}, u32[]{:S(2)}) collective-permute-start(bf16[2,1,2,256,256]{4,3,2,1,0:T(8,128)(2,1)} %get-tuple-element.160), channel_id=1, source_target_pairs={{0,2},{1,3},{2,0},{3,1},{4,6},{5,7},{6,4},{7,5},{8,10},{9,11},{10,... | collective-permute-start | bytes 1572872 | tf_op jit(solution)/shard_map/ppermute | solution.py:218
  43.4 19.4 %collective-permute-start.16 = (bf16[2,1,2,256,256]{4,3,2,1,0:T(8,128)(2,1)}, bf16[2,1,2,256,256]{4,3,2,1,0:T(8,128)(2,1)}, u32[]{:S(2)}, u32[]{:S(2)}) collective-permute-start(bf16[2,1,2,256,256]{4,3,2,1,0:T(8,128)(2,1)} %collective-permute-done.9.refs_3_), channel_id=1, source_target_pairs={{0,4},{1,5},{2,14},{3,15},{4,8},{5,9},{6,2},{7,3},{8,12},{9,13},{1... | collective-permute-start | bytes 1572872 | tf_op jit(solution)/shard_map/ppermute | solution.py:218
  44.9 20.9 %collective-permute-start.12 = (bf16[2,1,2,256,256]{4,3,2,1,0:T(8,128)(2,1)}, bf16[2,1,2,256,256]{4,3,2,1,0:T(8,128)(2,1)}, u32[]{:S(2)}, u32[]{:S(2)}) collective-permute-start(bf16[2,1,2,256,256]{4,3,2,1,0:T(8,128)(2,1)} %collective-permute-done.9.refs_3_), channel_id=1, source_target_pairs={{0,1},{1,0},{2,3},{3,2},{4,5},{5,4},{6,7},{7,6},{8,9},{9,8},{10,11... | collective-permute-start | bytes 1572872 | tf_op jit(solution)/shard_map/ppermute | solution.py:218
  51.6 14.2 %collective-permute-start.18 = (bf16[2,1,2,256,256]{4,3,2,1,0:T(8,128)(2,1)}, bf16[2,1,2,256,256]{4,3,2,1,0:T(8,128)(2,1)}, u32[]{:S(2)}, u32[]{:S(2)}) collective-permute-start(bf16[2,1,2,256,256]{4,3,2,1,0:T(8,128)(2,1)} %collective-permute-done.15.refs_10_), channel_id=1, source_target_pairs={{0,1},{1,0},{2,3},{3,2},{4,5},{5,4},{6,7},{7,6},{8,9},{9,8},{10,11... | collective-permute-start | bytes 1572872 | tf_op jit(solution)/shard_map/ppermute | solution.py:218
  52.2 13.6 %collective-permute-start.20 = (bf16[2,1,2,256,256]{4,3,2,1,0:T(8,128)(2,1)}, bf16[2,1,2,256,256]{4,3,2,1,0:T(8,128)(2,1)}, u32[]{:S(2)}, u32[]{:S(2)}) collective-permute-start(bf16[2,1,2,256,256]{4,3,2,1,0:T(8,128)(2,1)} %collective-permute-done.17.refs_12_), channel_id=1, source_target_pairs={{0,1},{1,0},{2,3},{3,2},{4,5},{5,4},{6,7},{7,6},{8,9},{9,8},{10,11... | collective-permute-start | bytes 1572872 | tf_op jit(solution)/shard_map/ppermute | solution.py:218
  56.2 9.6 %collective-permute-start.14 = (bf16[2,1,2,256,256]{4,3,2,1,0:T(8,128)(2,1)}, bf16[2,1,2,256,256]{4,3,2,1,0:T(8,128)(2,1)}, u32[]{:S(2)}, u32[]{:S(2)}) collective-permute-start(bf16[2,1,2,256,256]{4,3,2,1,0:T(8,128)(2,1)} %collective-permute-done.10.refs_5_), channel_id=1, source_target_pairs={{0,1},{1,0},{2,3},{3,2},{4,5},{5,4},{6,7},{7,6},{8,9},{9,8},{10,11... | collective-permute-start | bytes 1572872 | tf_op jit(solution)/shard_map/ppermute | solution.py:218
  62.9 2.9 %collective-permute-start.19 = (bf16[2,1,2,256,256]{4,3,2,1,0:T(8,128)(2,1)}, bf16[2,1,2,256,256]{4,3,2,1,0:T(8,128)(2,1)}, u32[]{:S(2)}, u32[]{:S(2)}) collective-permute-start(bf16[2,1,2,256,256]{4,3,2,1,0:T(8,128)(2,1)} %collective-permute-done.16.refs_11_), channel_id=1, source_target_pairs={{0,1},{1,0},{2,3},{3,2},{4,5},{5,4},{6,7},{7,6},{8,9},{9,8},{10,11... | collective-permute-start | bytes 1572872 | tf_op jit(solution)/shard_map/ppermute | solution.py:218
